TPU v7x, 128 devices: a whole 4x4x4 slice. The times are simulated.
128 devices in a mesh: cells: 128 (over z, y, x, core).
Axes of the slice: x: 4, y: 4, z: 4, core: 2. Of those that a mesh axis runs over, the one named last changes fastest.
Arguments:
- multipoles: bfloat16 [216, 131072], P(None, 'cells'), may hold values from -6 to 6
- compress: bfloat16 [216, 128], replicated, may hold values from -0.4375 to 0.4375
- operators: bfloat16 [316, 128, 128], replicated, may hold values from -0.0390625 to 0.0390625
- expand: bfloat16 [128, 216], replicated, may hold values from -0.5 to 0.5
Outputs:
- local_field: float32 [216, 131072], P(None, 'cells')
All inputs are finite; a program needn't handle non-finite values.
Results may differ from a plain program's by a relative error of at most 0.0041.
Values may be sent and summed in bfloat16 or wider, within the bound.
No kernel may reach another device: no remote copies, remote signals or barrier semaphores. Data moves between devices by JAX's collectives and lax.ppermute only.
A program may use at most 256 MiB of HBM per device.

v0:
```python
import functools

import jax
import jax.numpy as jnp
import numpy as np
from jax import lax
from jax.experimental import pallas as pl
from jax.experimental.pallas import tpu as pltpu
from jax.sharding import PartitionSpec as P

RANK = 128
BF = jnp.bfloat16
F32 = jnp.float32
OWN, X_ROWS, Y_ROWS, Z_ROWS = 128, 16, 48, 64
X_BASE = OWN
Y_BASE = X_BASE + 2 * X_ROWS
Z_BASE = Y_BASE + 2 * Y_ROWS
TABLE = Z_BASE + 2 * Z_ROWS
PIECES = 4
Y_TABLE, Z_TABLE, INNER_TABLE, OUTER_TABLE = 0, 96, 224, 736

OFFSETS = [
    (dx, dy, dz)
    for dx in range(-3, 4)
    for dy in range(-3, 4)
    for dz in range(-3, 4)
    if max(abs(dx), abs(dy), abs(dz)) >= 2
]
LOOKUP = {triple: number for number, triple in enumerate(OFFSETS)}
TARGETS = [(0, 0), (0, 1), (1, 0), (1, 1)]


def table_row(bits, sub):
    (x0, y0, z0), (sx, sy, sz) = bits, sub
    xi, yi = sx + x0, sy + y0
    if sz in (-1, 2):
        return Z_BASE + (sz == 2) * Z_ROWS + (x0 + 2 * y0) * 15 + xi + 5 * yi
    if sy in (-1, 2):
        return Y_BASE + (sy == 2) * Y_ROWS + (x0 + 2 * z0) * 10 + xi + 5 * sz
    if sx in (-1, 4):
        return X_BASE + (sx == 4) * X_ROWS + (y0 + 2 * z0) * 4 + sy + 2 * sz
    return (x0 + 2 * y0 + 4 * z0) * 16 + (sx & 1) + 2 * sy + 4 * sz + 8 * (sx >> 1)


def one_hot(sources, width):
    table = np.zeros((len(sources), width), np.float32)
    for row, source in enumerate(sources):
        if source is not None:
            table[row, source] = 1.0
    return table


def send_table(dimension, rows, width):
    top = (3, 1, 1)[dimension]
    result = [None] * (2 * rows)
    base = (X_BASE, Y_BASE, Z_BASE)[dimension]
    for upward in (1, 0):
        for number in range(8):
            bits = (number & 1, number >> 1 & 1, number >> 2 & 1)
            if bits[dimension] != upward:
                continue
            ranges = [range(-b, n + 1 - b) if d < dimension else range(n) for d, (b, n) in enumerate(zip(bits, (4, 2, 2)))]
            ranges[dimension] = [top if upward else 0]
            for sx in ranges[0]:
                for sy in ranges[1]:
                    for sz in ranges[2]:
                        here = [sx, sy, sz]
                        there = list(here)
                        there[dimension] = -1 if upward else top + 1
                        landing = table_row(bits, there) - base
                        assert landing // rows == 1 - upward
                        result[landing] = table_row(bits, here)
    return one_hot(result, width)


def window_table(planes):
    sources = []
    for px in range(4):
        for py in range(4):
            for pz in planes:
                for sb in range(16):
                    sub = ((sb & 1) + 2 * (sb >> 3), sb >> 1 & 1, sb >> 2 & 1)
                    place = [2 * s + p - 1 for s, p in zip(sub, (px, py, pz))]
                    sources.append(table_row([v & 1 for v in place], [v >> 1 for v in place]))
    return one_hot(sources, TABLE)


def matmul(a, b):
    return jnp.dot(a, b, preferred_element_type=F32)


def pick(even, sent, rows, to_even, to_odd):
    to_even[...] = sent[pl.ds(pl.multiple_of((1 - even) * rows, rows), rows), :]
    to_odd[...] = sent[pl.ds(pl.multiple_of(even * rows, rows), rows), :]


def place(even, from_even, from_odd, rows, landed):
    landed[pl.ds(pl.multiple_of(even * rows, rows), rows), :] = from_even[...]
    landed[pl.ds(pl.multiple_of((1 - even) * rows, rows), rows), :] = from_odd[...]


def x_picks():
    row = lax.broadcasted_iota(jnp.int32, (2 * X_ROWS, OWN), 0)
    column = lax.broadcasted_iota(jnp.int32, (2 * X_ROWS, OWN), 1)
    upward = 1 - (row >> 4)
    source = upward * 25 + (row >> 2 & 1) * 32 + (row >> 3 & 1) * 64 + (row & 1) * 2 + (row >> 1 & 1) * 4
    return jnp.where(column == source, 1.0, 0.0).astype(BF)


def compress_kernel(even, multipoles_hbm, compress_hbm, own, to_even, to_odd, multipoles, compress, rows, sent, sem):
    copies = [
        pltpu.make_async_copy(multipoles_hbm, multipoles, sem.at[0]),
        pltpu.make_async_copy(compress_hbm, compress, sem.at[1]),
    ]
    for copy in copies:
        copy.start()
    for copy in copies:
        copy.wait()
    rows[...] = lax.dot_general(
        multipoles[...], compress[...], (((0,), (0,)), ((), ())), preferred_element_type=F32
    )
    for number in range(8):
        for child in range(8):
            x0, y0, z0 = child & 1, child >> 1 & 1, child >> 2 & 1
            lane = ((x0 * 2 + y0) * 2 + z0) * RANK
            own[number * 16 : number * 16 + 16, lane : lane + RANK] = rows[
                pl.ds(number * 8 + child, 16, stride=64), :
            ].astype(BF)
    sent[...] = matmul(x_picks(), own[...]).astype(BF)
    pick(even[0], sent, X_ROWS, to_even, to_odd)


def stage_kernel(own, ops_hbm, table_hbm, ops, table, token, sem):
    pieces = [(table_hbm, table)]
    size = ops.shape[0] // PIECES
    for piece in range(PIECES):
        here = pl.ds(piece * size, size)
        pieces.append((ops_hbm.at[here], ops.at[here]))
    copies = [pltpu.make_async_copy(*piece, sem.at[i]) for i, piece in enumerate(pieces)]
    for copy in copies:
        copy.start()
    token[...] = jnp.zeros_like(token)
    for copy in copies:
        copy.wait()


def forward(table, own, landed, sent):
    rows, width = sent.shape[0], OWN + landed.shape[0]
    picks = table[:rows, :width]
    sent[...] = (matmul(picks[:, :OWN], own[...]) + matmul(picks[:, OWN:], landed[...])).astype(BF)


def forward_y_kernel(even, own, xe, xo, table, token, to_even, to_odd, landed, sent):
    place(even[0], xe, xo, X_ROWS, landed)
    forward(table.at[Y_TABLE:Z_TABLE], own, landed, sent)
    pick(even[1], sent, Y_ROWS, to_even, to_odd)


def forward_z_kernel(even, own, xe, xo, ye, yo, table, to_even, to_odd, landed, sent):
    place(even[0], xe, xo, X_ROWS, landed.at[0 : 2 * X_ROWS])
    place(even[1], ye, yo, Y_ROWS, landed.at[2 * X_ROWS :])
    forward(table.at[Z_TABLE:INNER_TABLE], own, landed, sent)
    pick(even[2], sent, Z_ROWS, to_even, to_odd)


def parity_shift(parity, distance):
    total = parity + distance
    return (total & 1, total >> 1) if abs(total >> 1) <= 1 else None


def operator_tiles(ops, dx, dy):
    base = LOOKUP[(dx, dy, -3)] * RANK
    if max(abs(dx), abs(dy)) >= 2:
        return [
            jnp.concatenate(
                [ops[first + RANK : first + 3 * RANK, :], ops[first : first + 2 * RANK, :]], axis=1
            )
            for first in (base, base + 2 * RANK, base + 4 * RANK)
        ]
    zero = jnp.zeros((RANK, RANK), BF)
    op = {dz: ops[base + i * RANK : base + (i + 1) * RANK, :] for i, dz in enumerate((-3, -2, 2, 3))}
    below = jnp.concatenate(
        [jnp.concatenate([op[-2], op[-3]], axis=1), jnp.concatenate([zero, op[-2]], axis=1)], axis=0
    )
    above = jnp.concatenate(
        [jnp.concatenate([op[2], zero], axis=1), jnp.concatenate([op[3], op[2]], axis=1)], axis=0
    )
    return [below, None, above]


def accumulate(window, ops, half, plane_of, pairs, targets, distances):
    total = None
    for dx, dy in distances:
        tiles = operator_tiles(ops, dx, dy)
        for pair in pairs:
            if tiles[pair] is None:
                continue
            parts = []
            for target in targets:
                (qx, cx), (qy, cy) = parity_shift(target[0], dx), parity_shift(target[1], dy)
                lane = (qx * 2 + qy) * 2 * RANK
                parts.append(
                    window[
                        1 + cx : 3 + cx, 1 + cy : 3 + cy, plane_of[half + pair], :, lane : lane + 2 * RANK
                    ].reshape(64, 2 * RANK)
                )
            left = jnp.concatenate(parts, axis=0) if len(parts) > 1 else parts[0]
            term = matmul(left, tiles[pair])
            total = term if total is None else total + term
    return total


def interact(window, ops, before, after, half, plane_of, pairs):
    def add(targets, distances, start):
        total = accumulate(window, ops, half, plane_of, pairs, targets, distances)
        for i, target in enumerate(targets):
            number = TARGETS.index(target)
            part = total[i * 64 : i * 64 + 64]
            after[half, number] = part if start is None else start[half, number] + part

    inner = range(-2, 3)
    add(TARGETS, [(dx, dy) for dx in inner for dy in inner], before)
    for p in (0, 1):
        far = 3 - 6 * p
        add([(p, 0), (p, 1)], [(far, dy) for dy in inner], after)
        add([(0, p), (1, p)], [(dx, far) for dx in inner], after)
    for x0, y0 in TARGETS:
        add([(x0, y0)], [(3 - 6 * x0, 3 - 6 * y0)], after)


def fill(window, table, first, own, landed, width):
    for px in range(4):
        block = table[first + px * 128 : first + px * 128 + 128, :width]
        filled = matmul(block[:, :OWN], own[...]) + matmul(block[:, OWN:], landed[...])
        window[px] = filled.astype(BF).reshape(4, 2, 16, 8 * RANK)


def inner_kernel(even, own, xe, xo, ye, yo, table, expand, ops, acc, outer, expand_out, landed, window):
    expand_out[...] = expand[...]
    place(even[0], xe, xo, X_ROWS, landed.at[0 : 2 * X_ROWS])
    place(even[1], ye, yo, Y_ROWS, landed.at[2 * X_ROWS :])
    fill(window, table, INNER_TABLE, own, landed, Z_BASE)
    fill(outer, table, OUTER_TABLE, own, landed, Z_BASE)
    planes = {1: 0, 2: 1}
    interact(window, ops, None, acc, 0, planes, (1, 2))
    interact(window, ops, None, acc, 1, planes, (0, 1))


def outer_kernel(even, ze, zo, table, expand, ops, inner, partial, out, landed, window, acc, rows):
    place(even[2], ze, zo, Z_ROWS, landed)
    for px in range(4):
        block = table[OUTER_TABLE + px * 128 : OUTER_TABLE + px * 128 + 128, Z_BASE:]
        filled = matmul(block, landed[...]) + partial[px].reshape(128, 8 * RANK).astype(F32)
        window[px] = filled.astype(BF).reshape(4, 2, 16, 8 * RANK)
    planes = {0: 0, 3: 1}
    interact(window, ops, inner, acc, 0, planes, (0,))
    interact(window, ops, inner, acc, 1, planes, (2,))
    for number in range(8):
        first = ((number & 1) * 2 + (number >> 1 & 1)) * 16
        for child in range(8):
            x0, y0, z0 = child & 1, child >> 1 & 1, child >> 2 & 1
            rows[pl.ds(number * 8 + child, 16, stride=64), :] = acc[
                number >> 2, x0 * 2 + y0, first : first + 16, z0 * RANK : z0 * RANK + RANK
            ]
    out[...] = lax.dot_general(
        expand[...], rows[...].astype(BF), (((1,), (1,)), ((), ())), preferred_element_type=F32
    )


VMEM = pl.BlockSpec(memory_space=pltpu.VMEM)
ANY = pl.BlockSpec(memory_space=pl.ANY)
SMEM = pl.BlockSpec(memory_space=pltpu.SMEM)


def rows_of(count):
    return jax.ShapeDtypeStruct((count, 8 * RANK), BF)


def in_hbm(array):
    return pltpu.with_memory_space_constraint(array, pltpu.HBM)


def scratch(*shape, kind=BF):
    return pltpu.VMEM(shape, kind)


def call(kernel, out_shape, scratch_shapes, in_specs, limit=16 << 20, flops=1 << 24, bytes_moved=1 << 20):
    return pl.pallas_call(
        kernel,
        out_shape=out_shape,
        in_specs=in_specs,
        out_specs=jax.tree.map(lambda _: VMEM, out_shape),
        scratch_shapes=scratch_shapes,
        compiler_params=pltpu.CompilerParams(vmem_limit_bytes=limit),
        cost_estimate=pl.CostEstimate(flops=flops, bytes_accessed=bytes_moved, transcendentals=0),
    )


def swap(blocks, bit_list, device_count):
    def position(device):
        return sum((device >> bit & 1) << rank for rank, bit in enumerate(bit_list))

    def move(device, new):
        for rank, bit in enumerate(bit_list):
            device = device & ~(1 << bit) | (new >> rank & 1) << bit
        return device

    extent = 1 << len(bit_list)
    result = []
    for parity, block in enumerate(blocks):
        route = []
        for device in range(device_count):
            at = position(device)
            partner = at + 1 if at % 2 == parity else at - 1
            if 0 <= partner < extent:
                route.append((device, move(device, partner)))
        result.append(lax.ppermute(block, "cells", route))
    return result


def local(multipoles, compress, operators, expand):
    local_bits = multipoles.shape[1].bit_length() - 1
    device_count = lax.axis_size("cells")
    bit_lists = [
        [bit for bit in range(device_count.bit_length() - 1) if (local_bits + bit) % 3 == dimension]
        for dimension in range(3)
    ]
    device = lax.axis_index("cells")
    even = jnp.stack([1 - (device >> bits[0] & 1) for bits in bit_lists]).astype(jnp.int32)

    pair = lambda count: [rows_of(count)] * 2
    tables = [
        send_table(1, Y_ROWS, TABLE),
        send_table(2, Z_ROWS, TABLE),
        window_table((1, 2)),
        window_table((0, 3)),
    ]
    table = jnp.asarray(np.concatenate(tables), BF)
    flat = operators.reshape(-1, RANK)
    own, *send = call(
        compress_kernel,
        [pltpu.VMEM((OWN, 8 * RANK), BF)] + pair(X_ROWS),
        [
            scratch(*multipoles.shape),
            scratch(*compress.shape),
            scratch(1024, RANK, kind=F32),
            scratch(2 * X_ROWS, 8 * RANK),
            pltpu.SemaphoreType.DMA((2,)),
        ],
        [SMEM] + [ANY] * 2,
    )(even, in_hbm(multipoles), in_hbm(compress))
    x_pair = swap(send, bit_lists[0], device_count)
    ops, table, token = call(
        stage_kernel,
        [
            pltpu.VMEM(flat.shape, BF),
            pltpu.VMEM(table.shape, BF),
            pltpu.VMEM((8, RANK), F32),
        ],
        [pltpu.SemaphoreType.DMA((1 + PIECES,))],
        [VMEM, ANY, ANY],
        bytes_moved=flat.size * 4,
    )(own, in_hbm(flat), in_hbm(table))
    send = call(
        forward_y_kernel,
        pair(Y_ROWS),
        [scratch(2 * X_ROWS, 8 * RANK), scratch(2 * Y_ROWS, 8 * RANK)],
        [SMEM] + [VMEM] * 5,
    )(even, own, *x_pair, table, token)
    y_pair = swap(send, bit_lists[1], device_count)
    send = call(
        forward_z_kernel,
        pair(Z_ROWS),
        [scratch(Z_BASE - OWN, 8 * RANK), scratch(2 * Z_ROWS, 8 * RANK)],
        [SMEM] + [VMEM] * 6,
    )(even, own, *x_pair, *y_pair, table)
    z_pair = swap(send, bit_lists[2], device_count)
    window = (4, 4, 2, 16, 8 * RANK)
    sums = (2, 4, 64, 2 * RANK)
    inner, partial, expand_t = call(
        inner_kernel,
        [
            pltpu.VMEM(sums, F32),
            pltpu.VMEM(window, BF),
            pltpu.VMEM(expand.shape[::-1], BF),
        ],
        [scratch(Z_BASE - OWN, 8 * RANK), scratch(*window)],
        [SMEM] + [VMEM] * 8,
        flops=5 << 30,
    )(even, own, *x_pair, *y_pair, table, expand.T, ops)
    return call(
        outer_kernel,
        jax.ShapeDtypeStruct((expand.shape[1], multipoles.shape[1]), F32),
        [
            scratch(2 * Z_ROWS, 8 * RANK),
            scratch(*window),
            scratch(*sums, kind=F32),
            scratch(1024, RANK, kind=F32),
        ],
        [SMEM] + [VMEM] * 7,
        flops=2 << 30,
    )(even, *z_pair, table, expand_t, ops, inner, partial)


def solution(mesh):
    placed = (P(None, "cells"), P(), P(), P())
    return jax.shard_map(
        local, mesh=mesh, in_specs=placed, out_specs=P(None, "cells"), check_vma=False
    )
```

profile of v0, /device:TPU:70, one launch (start us, length us, event | category | flops | bytes accessed | tf_op | source)
XLA Modules:
  0.0 41.6 jit_solution(9983473159644878987)
XLA Ops:
  0.0 0.0 copy-start
  0.0 0.1 pad_add_fusion.even
  0.1 2.4 %shard_map.55 = (bf16[128,1024]{1,0:T(8,128)(2,1)S(1)}, bf16[16,1024]{1,0:T(8,128)(2,1)S(1)}, bf16[16,1024]{1,0:T(8,128)(2,1)S(1)}) custom-call(s32[3]{0:T(128)S(1)} %pad_add_fusion.even, bf16[216,1024]{1,0:T(8,128)(2,1)} %multipoles_hbm.1, bf16[216,128]{1,0:T(8,128)(2,1)} %compress_hbm.1), custom_call_target="tpu_custom_call" | custom-call | flops 16777216 | bytes 1048576 | tf_op jit(solution)/shard_map/pallas_call | solution.py:340
  2.5 1.5 %collective-permute-start = (bf16[16,1024]{1,0:T(8,128)(2,1)S(1)}, bf16[16,1024]{1,0:T(8,128)(2,1)S(1)}, u32[]{:S(2)}, u32[]{:S(2)}) collective-permute-start(bf16[16,1024]{1,0:T(8,128)(2,1)S(1)} %get-tuple-element.19), channel_id=1, source_target_pairs={{0,4},{1,5},{2,6},{3,7},{4,0},{5,1},{6,2},{7,3},{8,12},{9,13},{10,... | collective-permute-start | bytes 98312 | tf_op jit(solution)/shard_map/ppermute | solution.py:317
  4.0 5.1 %collective-permute-start.1 = (bf16[16,1024]{1,0:T(8,128)(2,1)S(1)}, bf16[16,1024]{1,0:T(8,128)(2,1)S(1)}, u32[]{:S(2)}, u32[]{:S(2)}) collective-permute-start(bf16[16,1024]{1,0:T(8,128)(2,1)S(1)} %get-tuple-element.20), channel_id=1, source_target_pairs={{4,32},{5,33},{6,34},{7,35},{12,40},{13,41},{14,42},{15,43},{20,48... | collective-permute-start | bytes 98312 | tf_op jit(solution)/shard_map/ppermute | solution.py:317
  9.1 4.4 %shard_map.56 = (bf16[40448,128]{1,0:T(8,128)(2,1)S(1)}, bf16[1248,384]{1,0:T(8,128)(2,1)S(1)}, f32[8,128]{1,0:T(8,128)S(1)}) custom-call(bf16[128,1024]{1,0:T(8,128)(2,1)S(1)} %get-tuple-element.18.own, bf16[40448,128]{1,0:T(8,128)(2,1)} %bitcast.6, bf16[1248,384]{1,0:T(8,128)(2,1)} %constant.12.clone.table_hbm), custom_call_target="tpu_custom_call" | custom-call | flops 16777216 | bytes 20709376 | tf_op jit(solution)/shard_map/pallas_call | solution.py:353
  13.4 0.0 collective-permute-done.xe
  13.4 0.0 collective-permute-done.1.xo
  13.5 0.8 %shard_map.57 = (bf16[48,1024]{1,0:T(8,128)(2,1)S(1)}, bf16[48,1024]{1,0:T(8,128)(2,1)S(1)}) custom-call(s32[3]{0:T(128)S(1)} %pad_add_fusion.even, bf16[128,1024]{1,0:T(8,128)(2,1)S(1)} %get-tuple-element.18.own, bf16[16,1024]{1,0:T(8,128)(2,1)S(1)} %collective-permute-done.xe, bf16[16,1024]{1,0:T(8,128)(2,1)S(1)} %collective-permute-done.1.xo, ...), custom_call_target="tpu_custom_call" | custom-call | flops 16777216 | bytes 1048576 | tf_op jit(solution)/shard_map/pallas_call | solution.py:364
  14.3 0.1 collective-permute-start.2
  14.4 3.0 %collective-permute-start.3 = (bf16[48,1024]{1,0:T(8,128)(2,1)S(1)}, bf16[48,1024]{1,0:T(8,128)(2,1)S(1)}, u32[]{:S(2)}, u32[]{:S(2)}) collective-permute-start(bf16[48,1024]{1,0:T(8,128)(2,1)S(1)} %get-tuple-element.24), channel_id=1, source_target_pairs={{1,8},{3,10},{5,12},{7,14},{8,1},{9,64},{10,3},{11,66},{12,5},{13,... | collective-permute-start | bytes 294920 | tf_op jit(solution)/shard_map/ppermute | solution.py:317
  17.3 0.0 collective-permute-done.2.ye
  17.3 5.4 %collective-permute-done.3.yo = bf16[48,1024]{1,0:T(8,128)(2,1)S(1)} collective-permute-done((bf16[48,1024]{1,0:T(8,128)(2,1)S(1)}, bf16[48,1024]{1,0:T(8,128)(2,1)S(1)}, u32[]{:S(2)}, u32[]{:S(2)}) %collective-permute-start.3) | collective-permute-done | bytes 98336 | tf_op jit(solution)/shard_map/ppermute | solution.py:317
  22.7 0.9 %shard_map.58 = (bf16[64,1024]{1,0:T(8,128)(2,1)S(1)}, bf16[64,1024]{1,0:T(8,128)(2,1)S(1)}) custom-call(s32[3]{0:T(128)S(1)} %pad_add_fusion.even, bf16[128,1024]{1,0:T(8,128)(2,1)S(1)} %get-tuple-element.18.own, bf16[16,1024]{1,0:T(8,128)(2,1)S(1)} %collective-permute-done.xe, bf16[16,1024]{1,0:T(8,128)(2,1)S(1)} %collective-permute-done.1.xo, ...), custom_call_target="tpu_custom_call" | custom-call | flops 16777216 | bytes 1048576 | tf_op jit(solution)/shard_map/pallas_call | solution.py:371
  23.6 0.9 %collective-permute-start.4 = (bf16[64,1024]{1,0:T(8,128)(2,1)S(1)}, bf16[64,1024]{1,0:T(8,128)(2,1)S(1)}, u32[]{:S(2)}, u32[]{:S(2)}) collective-permute-start(bf16[64,1024]{1,0:T(8,128)(2,1)S(1)} %get-tuple-element.25), channel_id=1, source_target_pairs={{0,2},{1,3},{2,0},{3,1},{4,6},{5,7},{6,4},{7,5},{8,10},{9,11},{10,... | collective-permute-start | bytes 393224 | tf_op jit(solution)/shard_map/ppermute | solution.py:317
  24.5 5.7 %collective-permute-start.5 = (bf16[64,1024]{1,0:T(8,128)(2,1)S(1)}, bf16[64,1024]{1,0:T(8,128)(2,1)S(1)}, u32[]{:S(2)}, u32[]{:S(2)}) collective-permute-start(bf16[64,1024]{1,0:T(8,128)(2,1)S(1)} %get-tuple-element.26), channel_id=1, source_target_pairs={{2,16},{3,17},{6,20},{7,21},{10,24},{11,25},{14,28},{15,29},{16,2}... | collective-permute-start | bytes 393224 | tf_op jit(solution)/shard_map/ppermute | solution.py:317
  30.2 0.0 copy-done
  30.2 6.3 %shard_map.59 = (f32[2,4,64,256]{3,2,1,0:T(8,128)S(1)}, bf16[4,4,2,16,1024]{4,3,2,1,0:T(8,128)(2,1)S(1)}, bf16[216,128]{1,0:T(8,128)(2,1)S(1)}) custom-call(s32[3]{0:T(128)S(1)} %pad_add_fusion.even, bf16[128,1024]{1,0:T(8,128)(2,1)S(1)} %get-tuple-element.18.own, bf16[16,1024]{1,0:T(8,128)(2,1)S(1)} %collective-permute-done.xe, ...), custom_call_target="tpu_custom_call" | custom-call | flops 5368709120 | bytes 1048576 | tf_op jit(solution)/shard_map/pallas_call | solution.py:380
  36.5 0.0 collective-permute-done.4.ze
  36.5 0.0 collective-permute-done.5.zo
  36.5 5.0 %shard_map.60 = f32[216,1024]{1,0:T(8,128)} custom-call(s32[3]{0:T(128)S(1)} %pad_add_fusion.even, bf16[64,1024]{1,0:T(8,128)(2,1)S(1)} %collective-permute-done.4.ze, bf16[64,1024]{1,0:T(8,128)(2,1)S(1)} %collective-permute-done.5.zo, bf16[1248,384]{1,0:T(8,128)(2,1)S(1)} %get-tuple-element.21.table, bf16[216,128]{1,0:T(8,128)(2,1)S(1)} %get-tuple-element.28.expand, ...), custom_call_target="tpu_custom_call" | custom-call | flops 2147483648 | bytes 1048576 | tf_op jit(solution)/shard_map/pallas_call | solution.py:391
Async XLA Ops:
  0.0 30.2 %copy-start = (bf16[128,216]{0,1:T(8,128)(2,1)S(1)}, bf16[128,216]{0,1:T(8,128)(2,1)}, u32[]{:S(2)}) copy-start(bf16[128,216]{0,1:T(8,128)(2,1)} %param.8) | copy-start | bytes 165892
  2.5 10.9 %collective-permute-start = (bf16[16,1024]{1,0:T(8,128)(2,1)S(1)}, bf16[16,1024]{1,0:T(8,128)(2,1)S(1)}, u32[]{:S(2)}, u32[]{:S(2)}) collective-permute-start(bf16[16,1024]{1,0:T(8,128)(2,1)S(1)} %get-tuple-element.19), channel_id=1, source_target_pairs={{0,4},{1,5},{2,6},{3,7},{4,0},{5,1},{6,2},{7,3},{8,12},{9,13},{10,... | collective-permute-start | bytes 98312 | tf_op jit(solution)/shard_map/ppermute | solution.py:317
  4.0 9.5 %collective-permute-start.1 = (bf16[16,1024]{1,0:T(8,128)(2,1)S(1)}, bf16[16,1024]{1,0:T(8,128)(2,1)S(1)}, u32[]{:S(2)}, u32[]{:S(2)}) collective-permute-start(bf16[16,1024]{1,0:T(8,128)(2,1)S(1)} %get-tuple-element.20), channel_id=1, source_target_pairs={{4,32},{5,33},{6,34},{7,35},{12,40},{13,41},{14,42},{15,43},{20,48... | collective-permute-start | bytes 98312 | tf_op jit(solution)/shard_map/ppermute | solution.py:317
  14.3 3.1 %collective-permute-start.2 = (bf16[48,1024]{1,0:T(8,128)(2,1)S(1)}, bf16[48,1024]{1,0:T(8,128)(2,1)S(1)}, u32[]{:S(2)}, u32[]{:S(2)}) collective-permute-start(bf16[48,1024]{1,0:T(8,128)(2,1)S(1)} %get-tuple-element.23), channel_id=1, source_target_pairs={{0,1},{1,0},{2,3},{3,2},{4,5},{5,4},{6,7},{7,6},{8,9},{9,8},{10,11... | collective-permute-start | bytes 294920 | tf_op jit(solution)/shard_map/ppermute | solution.py:317
  14.4 8.3 %collective-permute-start.3 = (bf16[48,1024]{1,0:T(8,128)(2,1)S(1)}, bf16[48,1024]{1,0:T(8,128)(2,1)S(1)}, u32[]{:S(2)}, u32[]{:S(2)}) collective-permute-start(bf16[48,1024]{1,0:T(8,128)(2,1)S(1)} %get-tuple-element.24), channel_id=1, source_target_pairs={{1,8},{3,10},{5,12},{7,14},{8,1},{9,64},{10,3},{11,66},{12,5},{13,... | collective-permute-start | bytes 294920 | tf_op jit(solution)/shard_map/ppermute | solution.py:317
  23.6 12.9 %collective-permute-start.4 = (bf16[64,1024]{1,0:T(8,128)(2,1)S(1)}, bf16[64,1024]{1,0:T(8,128)(2,1)S(1)}, u32[]{:S(2)}, u32[]{:S(2)}) collective-permute-start(bf16[64,1024]{1,0:T(8,128)(2,1)S(1)} %get-tuple-element.25), channel_id=1, source_target_pairs={{0,2},{1,3},{2,0},{3,1},{4,6},{5,7},{6,4},{7,5},{8,10},{9,11},{10,... | collective-permute-start | bytes 393224 | tf_op jit(solution)/shard_map/ppermute | solution.py:317
  24.5 12.0 %collective-permute-start.5 = (bf16[64,1024]{1,0:T(8,128)(2,1)S(1)}, bf16[64,1024]{1,0:T(8,128)(2,1)S(1)}, u32[]{:S(2)}, u32[]{:S(2)}) collective-permute-start(bf16[64,1024]{1,0:T(8,128)(2,1)S(1)} %get-tuple-element.26), channel_id=1, source_target_pairs={{2,16},{3,17},{6,20},{7,21},{10,24},{11,25},{14,28},{15,29},{16,2}... | collective-permute-start | bytes 393224 | tf_op jit(solution)/shard_map/ppermute | solution.py:317
where the time goes:
time: 42.2 us; the launch traced here: 41.6 us
  Pallas kernels  19.7 us (47%)
  starting transfers between devices  16.3 us (39%)
  waiting for transfers between devices  5.38 us (13%)
    ppermute x6, starting transfers between devices, swap(): result.append(lax.ppermute(block, 'cells', route))  16.3 us
    pallas_call x1, Pallas kernels, local(): call(inner_kernel, [pltpu.VMEM(sums, F32), pltpu.VMEM(window, BF), pltpu....  6.27 us
    ppermute x6, waiting for transfers between devices, swap(): result.append(lax.ppermute(block, 'cells', route))  5.38 us
    pallas_call x1, Pallas kernels, local(): call(outer_kernel, jax.ShapeDtypeStruct((expand.shape[1], multipoles.shap...  5.05 us
    pallas_call x1, Pallas kernels, local(): call(stage_kernel, [pltpu.VMEM(flat.shape, BF), pltpu.VMEM(table.shape, B...  4.35 us
    pallas_call x1, Pallas kernels, local(): call(compress_kernel, [pltpu.VMEM((OWN, 8 * RANK), BF)] + pair(X_ROWS), [...  2.41 us
    pallas_call x1, Pallas kernels, local(): call(forward_z_kernel, pair(Z_ROWS), [scratch(Z_BASE - OWN, 8 * RANK), sc...  0.87 us
  transfers between devices with their start and end apart: 6, of which 1 were waited for; matrix products, arithmetic and copies ran while one was open for 0% of the time, Pallas kernels for 26%

commit v1 on v0

--- a/solution.py
+++ b/solution.py
@@ -17,7 +17,7 @@
 Z_BASE = Y_BASE + 2 * Y_ROWS
 TABLE = Z_BASE + 2 * Z_ROWS
 PIECES = 4
-Y_TABLE, Z_TABLE, INNER_TABLE, OUTER_TABLE = 0, 96, 224, 736
+Y_TABLE, Z_TABLE, LEVEL_TABLE, SIDE_TABLE, OUTER_TABLE, ORDER_TABLE = 0, 96, 224, 480, 992, 1376
 
 OFFSETS = [
     (dx, dy, dz)
@@ -73,15 +73,22 @@
     return one_hot(result, width)
 
 
-def window_table(planes):
+def window_table(rows_y, planes):
     sources = []
     for px in range(4):
-        for py in range(4):
+        for py in rows_y:
             for pz in planes:
-                for sb in range(16):
-                    sub = ((sb & 1) + 2 * (sb >> 3), sb >> 1 & 1, sb >> 2 & 1)
-                    place = [2 * s + p - 1 for s, p in zip(sub, (px, py, pz))]
+                for column in range(16):
+                    place = [2 * (column >> 2) + px - 1, (column & 3) + py - 1, pz - 1]
                     sources.append(table_row([v & 1 for v in place], [v >> 1 for v in place]))
+    return one_hot(sources, TABLE)
+
+
+def order_table():
+    sources = []
+    for parent in range(128):
+        x0, y0, z0, x1, y1, z1, x2 = [parent >> bit & 1 for bit in range(7)]
+        sources.append((z0 + 2 * z1) * 32 + x0 * 16 + (x1 + 2 * x2) * 4 + y0 + 2 * y1)
     return one_hot(sources, TABLE)
 
 
@@ -145,9 +152,8 @@
 
 
 def forward(table, own, landed, sent):
-    rows, width = sent.shape[0], OWN + landed.shape[0]
-    picks = table[:rows, :width]
-    sent[...] = (matmul(picks[:, :OWN], own[...]) + matmul(picks[:, OWN:], landed[...])).astype(BF)
+    width = OWN + landed.shape[0]
+    sent[...] = (matmul(table[:, :OWN], own[...]) + matmul(table[:, OWN:width], landed[...])).astype(BF)
 
 
 def forward_y_kernel(even, own, xe, xo, table, token, to_even, to_odd, landed, sent):
@@ -156,10 +162,10 @@
     pick(even[1], sent, Y_ROWS, to_even, to_odd)
 
 
-def forward_z_kernel(even, own, xe, xo, ye, yo, table, to_even, to_odd, landed, sent):
-    place(even[0], xe, xo, X_ROWS, landed.at[0 : 2 * X_ROWS])
+def forward_z_kernel(even, own, x_landed, yo, ye, table, token, to_even, to_odd, landed, sent):
+    landed[0 : 2 * X_ROWS] = x_landed[...]
     place(even[1], ye, yo, Y_ROWS, landed.at[2 * X_ROWS :])
-    forward(table.at[Z_TABLE:INNER_TABLE], own, landed, sent)
+    forward(table.at[Z_TABLE:LEVEL_TABLE], own, landed, sent)
     pick(even[2], sent, Z_ROWS, to_even, to_odd)
 
 
@@ -188,7 +194,7 @@
     return [below, None, above]
 
 
-def accumulate(window, ops, half, plane_of, pairs, targets, distances):
+def accumulate(source, ops, planes, pairs, targets, distances):
     total = None
     for dx, dy in distances:
         tiles = operator_tiles(ops, dx, dy)
@@ -196,72 +202,92 @@
             if tiles[pair] is None:
                 continue
             parts = []
-            for target in targets:
-                (qx, cx), (qy, cy) = parity_shift(target[0], dx), parity_shift(target[1], dy)
-                lane = (qx * 2 + qy) * 2 * RANK
-                parts.append(
-                    window[
-                        1 + cx : 3 + cx, 1 + cy : 3 + cy, plane_of[half + pair], :, lane : lane + 2 * RANK
-                    ].reshape(64, 2 * RANK)
-                )
+            for plane in planes:
+                for target in targets:
+                    (qx, cx), (qy, cy) = parity_shift(target[0], dx), parity_shift(target[1], dy)
+                    lane = (qx * 2 + qy) * 2 * RANK
+                    block = source(cx, cy, plane + pair, slice(lane, lane + 2 * RANK))
+                    parts.append(block.reshape(32, 2 * RANK))
             left = jnp.concatenate(parts, axis=0) if len(parts) > 1 else parts[0]
             term = matmul(left, tiles[pair])
             total = term if total is None else total + term
     return total
 
 
-def interact(window, ops, before, after, half, plane_of, pairs):
+def interact(source, ops, before, after, planes, pairs, shared, special):
     def add(targets, distances, start):
-        total = accumulate(window, ops, half, plane_of, pairs, targets, distances)
-        for i, target in enumerate(targets):
-            number = TARGETS.index(target)
-            part = total[i * 64 : i * 64 + 64]
-            after[half, number] = part if start is None else start[half, number] + part
-
-    inner = range(-2, 3)
-    add(TARGETS, [(dx, dy) for dx in inner for dy in inner], before)
-    for p in (0, 1):
-        far = 3 - 6 * p
-        add([(p, 0), (p, 1)], [(far, dy) for dy in inner], after)
-        add([(0, p), (1, p)], [(dx, far) for dx in inner], after)
+        total = accumulate(source, ops, planes, pairs, targets, distances)
+        for i, plane in enumerate(planes):
+            for j, target in enumerate(targets):
+                number = TARGETS.index(target)
+                first = (i * len(targets) + j) * 32
+                part = total[first : first + 32]
+                after[plane, number] = part if start is None else start[plane, number] + part
+
+    near, far = range(-2, 3), (3, -3)
+    add(TARGETS, [(dx, dy) for dx in near for dy in shared], before)
+    for x0 in (0, 1):
+        add([(x0, 0), (x0, 1)], [(far[x0], dy) for dy in shared], after)
+    for y0 in (0, 1):
+        add([(0, y0), (1, y0)], [(dx, dy) for dx in near for dy in special[y0]], after)
     for x0, y0 in TARGETS:
-        add([(x0, y0)], [(3 - 6 * x0, 3 - 6 * y0)], after)
-
-
-def fill(window, table, first, own, landed, width):
+        add([(x0, y0)], [(far[x0], dy) for dy in special[y0]], after)
+
+
+ALL_PLANES, ALL_PAIRS = range(4), range(3)
+
+
+def fill(window, table, own, landed):
+    width = OWN + landed.shape[0]
+    rows = table.shape[0] // 4
     for px in range(4):
-        block = table[first + px * 128 : first + px * 128 + 128, :width]
+        block = table[px * rows : px * rows + rows, :width]
         filled = matmul(block[:, :OWN], own[...]) + matmul(block[:, OWN:], landed[...])
-        window[px] = filled.astype(BF).reshape(4, 2, 16, 8 * RANK)
-
-
-def inner_kernel(even, own, xe, xo, ye, yo, table, expand, ops, acc, outer, expand_out, landed, window):
+        inside = filled.astype(BF).reshape(window.shape[1], 4, 16, 8 * RANK)
+        window[px, :, 1:5] = inside
+        window[px, :, 0:1] = jnp.zeros_like(inside[:, :1])
+        window[px, :, 5:6] = jnp.zeros_like(inside[:, :1])
+
+
+def level_kernel(own, landed, table, ops, acc, token, window):
+    token[...] = jnp.zeros_like(token)
+    fill(window, table.at[LEVEL_TABLE:SIDE_TABLE], own, landed)
+
+    def source(cx, cy, plane, lanes):
+        return window[1 + cx : 3 + cx, 0, plane, :, lanes]
+
+    interact(source, ops, None, acc, ALL_PLANES, ALL_PAIRS, [0], ([1], [-1]))
+
+
+def side_kernel(own, landed, table, expand, ops, level, acc, expand_out, window):
     expand_out[...] = expand[...]
-    place(even[0], xe, xo, X_ROWS, landed.at[0 : 2 * X_ROWS])
-    place(even[1], ye, yo, Y_ROWS, landed.at[2 * X_ROWS :])
-    fill(window, table, INNER_TABLE, own, landed, Z_BASE)
-    fill(outer, table, OUTER_TABLE, own, landed, Z_BASE)
-    planes = {1: 0, 2: 1}
-    interact(window, ops, None, acc, 0, planes, (1, 2))
-    interact(window, ops, None, acc, 1, planes, (0, 1))
-
-
-def outer_kernel(even, ze, zo, table, expand, ops, inner, partial, out, landed, window, acc, rows):
+    fill(window, table.at[SIDE_TABLE:OUTER_TABLE], own, landed)
+
+    def source(cx, cy, plane, lanes):
+        return window[1 + cx : 3 + cx, (cy + 1) // 2, plane, :, lanes]
+
+    interact(source, ops, level, acc, ALL_PLANES, ALL_PAIRS, [-2, 2], ([-1, 3], [-3, 1]))
+
+
+def outer_kernel(even, ze, zo, table, expand, ops, inner, out, landed, window, acc, rows):
     place(even[2], ze, zo, Z_ROWS, landed)
     for px in range(4):
-        block = table[OUTER_TABLE + px * 128 : OUTER_TABLE + px * 128 + 128, Z_BASE:]
-        filled = matmul(block, landed[...]) + partial[px].reshape(128, 8 * RANK).astype(F32)
-        window[px] = filled.astype(BF).reshape(4, 2, 16, 8 * RANK)
-    planes = {0: 0, 3: 1}
-    interact(window, ops, inner, acc, 0, planes, (0,))
-    interact(window, ops, inner, acc, 1, planes, (2,))
-    for number in range(8):
-        first = ((number & 1) * 2 + (number >> 1 & 1)) * 16
-        for child in range(8):
-            x0, y0, z0 = child & 1, child >> 1 & 1, child >> 2 & 1
-            rows[pl.ds(number * 8 + child, 16, stride=64), :] = acc[
-                number >> 2, x0 * 2 + y0, first : first + 16, z0 * RANK : z0 * RANK + RANK
-            ]
+        block = table[OUTER_TABLE + px * 96 : OUTER_TABLE + px * 96 + 96, Z_BASE:]
+        window[px] = matmul(block, landed[...]).astype(BF).reshape(window.shape[1:])
+
+    def source(cx, cy, plane, lanes):
+        return window[1 + cx : 3 + cx, 1 + cy, plane // 5, :, lanes]
+
+    for planes, pairs in (((0,), (0,)), ((3,), (2,))):
+        interact(source, ops, inner, acc, planes, pairs, range(-2, 3), ([3], [-3]))
+    order = table[ORDER_TABLE : ORDER_TABLE + 128, :128]
+    for number, (x0, y0) in enumerate(TARGETS):
+        whole = jnp.concatenate(
+            [(acc if plane in (0, 3) else inner)[plane, number].astype(BF) for plane in range(4)], axis=0
+        )
+        ordered = matmul(order, whole)
+        for z0 in (0, 1):
+            rows[pl.ds(x0 + 2 * y0 + 4 * z0, 128, stride=8), :] = ordered[:, z0 * RANK : z0 * RANK + RANK]
     out[...] = lax.dot_general(
         expand[...], rows[...].astype(BF), (((1,), (1,)), ((), ())), preferred_element_type=F32
     )
@@ -332,8 +358,10 @@
     tables = [
         send_table(1, Y_ROWS, TABLE),
         send_table(2, Z_ROWS, TABLE),
-        window_table((1, 2)),
-        window_table((0, 3)),
+        window_table((1,), range(1, 5)),
+        window_table((0, 2), range(1, 5)),
+        window_table(range(3), (0, 5)),
+        order_table(),
     ]
     table = jnp.asarray(np.concatenate(tables), BF)
     flat = operators.reshape(-1, RANK)
@@ -361,45 +389,47 @@
         [VMEM, ANY, ANY],
         bytes_moved=flat.size * 4,
     )(own, in_hbm(flat), in_hbm(table))
-    send = call(
+    *send, landed = call(
         forward_y_kernel,
-        pair(Y_ROWS),
-        [scratch(2 * X_ROWS, 8 * RANK), scratch(2 * Y_ROWS, 8 * RANK)],
+        pair(Y_ROWS) + [pltpu.VMEM((2 * X_ROWS, 8 * RANK), BF)],
+        [scratch(2 * Y_ROWS, 8 * RANK)],
         [SMEM] + [VMEM] * 5,
     )(even, own, *x_pair, table, token)
     y_pair = swap(send, bit_lists[1], device_count)
-    send = call(
+    sums = (4, 4, 32, 2 * RANK)
+    level, token = call(
+        level_kernel,
+        [pltpu.VMEM(sums, F32), pltpu.VMEM((8, RANK), F32)],
+        [scratch(4, 1, 6, 16, 8 * RANK)],
+        [VMEM] * 4,
+        flops=2 << 30,
+    )(own, landed, table, ops)
+    *send, landed = call(
         forward_z_kernel,
-        pair(Z_ROWS),
-        [scratch(Z_BASE - OWN, 8 * RANK), scratch(2 * Z_ROWS, 8 * RANK)],
+        pair(Z_ROWS) + [pltpu.VMEM((Z_BASE - OWN, 8 * RANK), BF)],
+        [scratch(2 * Z_ROWS, 8 * RANK)],
         [SMEM] + [VMEM] * 6,
-    )(even, own, *x_pair, *y_pair, table)
+    )(even, own, landed, *y_pair[::-1], table, token)
     z_pair = swap(send, bit_lists[2], device_count)
-    window = (4, 4, 2, 16, 8 * RANK)
-    sums = (2, 4, 64, 2 * RANK)
-    inner, partial, expand_t = call(
-        inner_kernel,
-        [
-            pltpu.VMEM(sums, F32),
-            pltpu.VMEM(window, BF),
-            pltpu.VMEM(expand.shape[::-1], BF),
-        ],
-        [scratch(Z_BASE - OWN, 8 * RANK), scratch(*window)],
-        [SMEM] + [VMEM] * 8,
+    inner, expand_t = call(
+        side_kernel,
+        [pltpu.VMEM(sums, F32), pltpu.VMEM(expand.shape[::-1], BF)],
+        [scratch(4, 2, 6, 16, 8 * RANK)],
+        [VMEM] * 6,
         flops=5 << 30,
-    )(even, own, *x_pair, *y_pair, table, expand.T, ops)
+    )(own, landed, table, expand.T, ops, level)
     return call(
         outer_kernel,
         jax.ShapeDtypeStruct((expand.shape[1], multipoles.shape[1]), F32),
         [
             scratch(2 * Z_ROWS, 8 * RANK),
-            scratch(*window),
+            scratch(4, 3, 2, 16, 8 * RANK),
             scratch(*sums, kind=F32),
             scratch(1024, RANK, kind=F32),
         ],
-        [SMEM] + [VMEM] * 7,
+        [SMEM] + [VMEM] * 6,
         flops=2 << 30,
-    )(even, *z_pair, table, expand_t, ops, inner, partial)
+    )(even, *z_pair, table, expand_t, ops, inner)
 
 
 def solution(mesh):

time: 42.2 us -> 40 us (0.948); the launches traced: 41.6 us -> 39.9 us
  waiting for transfers between devices: 5.38 us -> 2.17 us
  Pallas kernels: 19.7 us -> 20.6 us
  starting transfers between devices: 16.3 us -> 16.9 us
    ppermute x6, waiting for transfers between devices: 5.38 us -> 2.17 us  [swap(): result.append(lax.ppermute(block, 'cells', route))]
    pallas_call x3 -> x4, Pallas kernels: 7.94 us -> 9.55 us  [the longest x1 5.39 us: local(): call(side_kernel, [pltpu.VMEM(sums, F32), pltpu.VMEM(expand.shape[::-1],...]
    pallas_call x1, Pallas kernels: 5.05 us -> 4.24 us  [local(): call(outer_kernel, jax.ShapeDtypeStruct((expand.shape[1], multipoles.shap...]
    ppermute x6, starting transfers between devices: 16.3 us -> 16.9 us  [swap(): result.append(lax.ppermute(block, 'cells', route))]
  transfers between devices with their start and end apart: 6 -> 6, of which waited for: 1 -> 1; matrix products, arithmetic and copies ran while one was open for 0% -> 0% of each run, Pallas kernels for 26% -> 31%
where the time goes in v1:
time: 40 us; the launch traced here: 39.9 us
  Pallas kernels  20.6 us (52%)
  starting transfers between devices  16.9 us (42%)
  waiting for transfers between devices  2.17 us (5%)
    ppermute x6, starting transfers between devices, swap(): result.append(lax.ppermute(block, 'cells', route))  16.9 us
    pallas_call x1, Pallas kernels, local(): call(side_kernel, [pltpu.VMEM(sums, F32), pltpu.VMEM(expand.shape[::-1],...  5.39 us
    pallas_call x1, Pallas kernels, local(): call(stage_kernel, [pltpu.VMEM(flat.shape, BF), pltpu.VMEM(table.shape, B...  4.41 us
    pallas_call x1, Pallas kernels, local(): call(outer_kernel, jax.ShapeDtypeStruct((expand.shape[1], multipoles.shap...  4.24 us
    pallas_call x1, Pallas kernels, local(): call(level_kernel, [pltpu.VMEM(sums, F32), pltpu.VMEM((8, RANK), F32)], [...  2.48 us
    pallas_call x1, Pallas kernels, local(): call(compress_kernel, [pltpu.VMEM((OWN, 8 * RANK), BF)] + pair(X_ROWS), [...  2.41 us
    ppermute x6, waiting for transfers between devices, swap(): result.append(lax.ppermute(block, 'cells', route))  2.17 us
    pallas_call x1, Pallas kernels, local(): call(forward_z_kernel, pair(Z_ROWS) + [pltpu.VMEM((Z_BASE - OWN, 8 * RANK...  0.86 us
  transfers between devices with their start and end apart: 6, of which 1 were waited for; matrix products, arithmetic and copies ran while one was open for 0% of the time, Pallas kernels for 31%

profile of v1, /device:TPU:70, one launch (start us, length us, event | category | flops | bytes accessed | tf_op | source)
XLA Modules:
  0.0 39.9 jit_solution(1515824943952881560)
XLA Ops:
  0.0 0.1 pad_add_fusion.even
  0.1 2.4 %shard_map.55 = (bf16[128,1024]{1,0:T(8,128)(2,1)S(1)}, bf16[16,1024]{1,0:T(8,128)(2,1)S(1)}, bf16[16,1024]{1,0:T(8,128)(2,1)S(1)}) custom-call(s32[3]{0:T(128)S(1)} %pad_add_fusion.even, bf16[216,1024]{1,0:T(8,128)(2,1)} %multipoles_hbm.1, bf16[216,128]{1,0:T(8,128)(2,1)} %compress_hbm.1), custom_call_target="tpu_custom_call" | custom-call | flops 16777216 | bytes 1048576 | tf_op jit(solution)/shard_map/pallas_call | solution.py:368
  2.5 1.5 %collective-permute-start = (bf16[16,1024]{1,0:T(8,128)(2,1)S(1)}, bf16[16,1024]{1,0:T(8,128)(2,1)S(1)}, u32[]{:S(2)}, u32[]{:S(2)}) collective-permute-start(bf16[16,1024]{1,0:T(8,128)(2,1)S(1)} %get-tuple-element.22), channel_id=1, source_target_pairs={{0,4},{1,5},{2,6},{3,7},{4,0},{5,1},{6,2},{7,3},{8,12},{9,13},{10,... | collective-permute-start | bytes 98312 | tf_op jit(solution)/shard_map/ppermute | solution.py:343
  4.0 5.1 %collective-permute-start.1 = (bf16[16,1024]{1,0:T(8,128)(2,1)S(1)}, bf16[16,1024]{1,0:T(8,128)(2,1)S(1)}, u32[]{:S(2)}, u32[]{:S(2)}) collective-permute-start(bf16[16,1024]{1,0:T(8,128)(2,1)S(1)} %get-tuple-element.23), channel_id=1, source_target_pairs={{4,32},{5,33},{6,34},{7,35},{12,40},{13,41},{14,42},{15,43},{20,48... | collective-permute-start | bytes 98312 | tf_op jit(solution)/shard_map/ppermute | solution.py:343
  9.1 4.4 %shard_map.56 = (bf16[40448,128]{1,0:T(8,128)(2,1)S(1)}, bf16[1504,384]{1,0:T(8,128)(2,1)S(1)}, f32[8,128]{1,0:T(8,128)S(1)}) custom-call(bf16[128,1024]{1,0:T(8,128)(2,1)S(1)} %get-tuple-element.21.own, bf16[40448,128]{1,0:T(8,128)(2,1)} %bitcast.6, bf16[1504,384]{1,0:T(8,128)(2,1)} %constant.12.clone.table_hbm), custom_call_target="tpu_custom_call" | custom-call | flops 16777216 | bytes 20709376 | tf_op jit(solution)/shard_map/pallas_call | solution.py:381
  13.5 0.0 copy-start
  13.5 0.0 collective-permute-done.xe
  13.5 0.0 collective-permute-done.1.xo
  13.5 0.8 %shard_map.57 = (bf16[48,1024]{1,0:T(8,128)(2,1)S(1)}, bf16[48,1024]{1,0:T(8,128)(2,1)S(1)}, bf16[32,1024]{1,0:T(8,128)(2,1)S(1)}) custom-call(s32[3]{0:T(128)S(1)} %pad_add_fusion.even, bf16[128,1024]{1,0:T(8,128)(2,1)S(1)} %get-tuple-element.21.own, bf16[16,1024]{1,0:T(8,128)(2,1)S(1)} %collective-permute-done.xe, ...), custom_call_target="tpu_custom_call" | custom-call | flops 16777216 | bytes 1048576 | tf_op jit(solution)/shard_map/pallas_call | solution.py:392
  14.3 1.9 %collective-permute-start.2 = (bf16[48,1024]{1,0:T(8,128)(2,1)S(1)}, bf16[48,1024]{1,0:T(8,128)(2,1)S(1)}, u32[]{:S(2)}, u32[]{:S(2)}) collective-permute-start(bf16[48,1024]{1,0:T(8,128)(2,1)S(1)} %get-tuple-element.27), channel_id=1, source_target_pairs={{1,8},{3,10},{5,12},{7,14},{8,1},{9,64},{10,3},{11,66},{12,5},{13,... | collective-permute-start | bytes 294920 | tf_op jit(solution)/shard_map/ppermute | solution.py:343
  16.3 1.8 %collective-permute-start.3 = (bf16[48,1024]{1,0:T(8,128)(2,1)S(1)}, bf16[48,1024]{1,0:T(8,128)(2,1)S(1)}, u32[]{:S(2)}, u32[]{:S(2)}) collective-permute-start(bf16[48,1024]{1,0:T(8,128)(2,1)S(1)} %get-tuple-element.28), channel_id=1, source_target_pairs={{0,1},{1,0},{2,3},{3,2},{4,5},{5,4},{6,7},{7,6},{8,9},{9,8},{10,11... | collective-permute-start | bytes 294920 | tf_op jit(solution)/shard_map/ppermute | solution.py:343
  18.0 2.5 %shard_map.58 = (f32[4,4,32,256]{3,2,1,0:T(8,128)S(1)}, f32[8,128]{1,0:T(8,128)S(1)}) custom-call(bf16[128,1024]{1,0:T(8,128)(2,1)S(1)} %get-tuple-element.21.own, bf16[32,1024]{1,0:T(8,128)(2,1)S(1)} %get-tuple-element.26.landed.x_landed, bf16[1504,384]{1,0:T(8,128)(2,1)S(1)} %get-tuple-element.24.table, bf16[40448,128]{1,0:T(8,128)(2,1)S(1)} %get-tuple-element.29.ops), custom_call_target="tpu_custom_call" | custom-call | flops 2147483648 | bytes 1048576 | tf_op jit(solution)/shard_map/pallas_call | solution.py:400
  20.5 2.2 %collective-permute-done.2.yo = bf16[48,1024]{1,0:T(8,128)(2,1)S(1)} collective-permute-done((bf16[48,1024]{1,0:T(8,128)(2,1)S(1)}, bf16[48,1024]{1,0:T(8,128)(2,1)S(1)}, u32[]{:S(2)}, u32[]{:S(2)}) %collective-permute-start.2) | collective-permute-done | bytes 98336 | tf_op jit(solution)/shard_map/ppermute | solution.py:343
  22.7 0.0 collective-permute-done.3.ye
  22.7 0.9 %shard_map.59 = (bf16[64,1024]{1,0:T(8,128)(2,1)S(1)}, bf16[64,1024]{1,0:T(8,128)(2,1)S(1)}, bf16[128,1024]{1,0:T(8,128)(2,1)S(1)}) custom-call(s32[3]{0:T(128)S(1)} %pad_add_fusion.even, bf16[128,1024]{1,0:T(8,128)(2,1)S(1)} %get-tuple-element.21.own, bf16[32,1024]{1,0:T(8,128)(2,1)S(1)} %get-tuple-element.26.landed.x_landed, ...), custom_call_target="tpu_custom_call" | custom-call | flops 16777216 | bytes 1048576 | tf_op jit(solution)/shard_map/pallas_call | solution.py:407
  23.6 0.9 %collective-permute-start.4 = (bf16[64,1024]{1,0:T(8,128)(2,1)S(1)}, bf16[64,1024]{1,0:T(8,128)(2,1)S(1)}, u32[]{:S(2)}, u32[]{:S(2)}) collective-permute-start(bf16[64,1024]{1,0:T(8,128)(2,1)S(1)} %get-tuple-element.31), channel_id=1, source_target_pairs={{0,2},{1,3},{2,0},{3,1},{4,6},{5,7},{6,4},{7,5},{8,10},{9,11},{10,... | collective-permute-start | bytes 393224 | tf_op jit(solution)/shard_map/ppermute | solution.py:343
  24.4 5.7 %collective-permute-start.5 = (bf16[64,1024]{1,0:T(8,128)(2,1)S(1)}, bf16[64,1024]{1,0:T(8,128)(2,1)S(1)}, u32[]{:S(2)}, u32[]{:S(2)}) collective-permute-start(bf16[64,1024]{1,0:T(8,128)(2,1)S(1)} %get-tuple-element.32), channel_id=1, source_target_pairs={{2,16},{3,17},{6,20},{7,21},{10,24},{11,25},{14,28},{15,29},{16,2}... | collective-permute-start | bytes 393224 | tf_op jit(solution)/shard_map/ppermute | solution.py:343
  30.2 0.0 copy-done
  30.2 5.4 %shard_map.60 = (f32[4,4,32,256]{3,2,1,0:T(8,128)S(1)}, bf16[216,128]{1,0:T(8,128)(2,1)S(1)}) custom-call(bf16[128,1024]{1,0:T(8,128)(2,1)S(1)} %get-tuple-element.21.own, bf16[128,1024]{1,0:T(8,128)(2,1)S(1)} %get-tuple-element.33.landed, bf16[1504,384]{1,0:T(8,128)(2,1)S(1)} %get-tuple-element.24.table, bf16[216,128]{1,0:T(8,128)(2,1)S(1)} %bitcast.5, ...), custom_call_target="tpu_custom_call" | custom-call | flops 5368709120 | bytes 1048576 | tf_op jit(solution)/shard_map/pallas_call | solution.py:414
  35.6 0.0 collective-permute-done.4.ze
  35.6 0.0 collective-permute-done.5.zo
  35.6 4.2 %shard_map.61 = f32[216,1024]{1,0:T(8,128)} custom-call(s32[3]{0:T(128)S(1)} %pad_add_fusion.even, bf16[64,1024]{1,0:T(8,128)(2,1)S(1)} %collective-permute-done.4.ze, bf16[64,1024]{1,0:T(8,128)(2,1)S(1)} %collective-permute-done.5.zo, bf16[1504,384]{1,0:T(8,128)(2,1)S(1)} %get-tuple-element.24.table, bf16[216,128]{1,0:T(8,128)(2,1)S(1)} %get-tuple-element.35.expand, ...), custom_call_target="tpu_custom_call" | custom-call | flops 2147483648 | bytes 1048576 | tf_op jit(solution)/shard_map/pallas_call | solution.py:421
Async XLA Ops:
  2.5 11.0 %collective-permute-start = (bf16[16,1024]{1,0:T(8,128)(2,1)S(1)}, bf16[16,1024]{1,0:T(8,128)(2,1)S(1)}, u32[]{:S(2)}, u32[]{:S(2)}) collective-permute-start(bf16[16,1024]{1,0:T(8,128)(2,1)S(1)} %get-tuple-element.22), channel_id=1, source_target_pairs={{0,4},{1,5},{2,6},{3,7},{4,0},{5,1},{6,2},{7,3},{8,12},{9,13},{10,... | collective-permute-start | bytes 98312 | tf_op jit(solution)/shard_map/ppermute | solution.py:343
  4.0 9.5 %collective-permute-start.1 = (bf16[16,1024]{1,0:T(8,128)(2,1)S(1)}, bf16[16,1024]{1,0:T(8,128)(2,1)S(1)}, u32[]{:S(2)}, u32[]{:S(2)}) collective-permute-start(bf16[16,1024]{1,0:T(8,128)(2,1)S(1)} %get-tuple-element.23), channel_id=1, source_target_pairs={{4,32},{5,33},{6,34},{7,35},{12,40},{13,41},{14,42},{15,43},{20,48... | collective-permute-start | bytes 98312 | tf_op jit(solution)/shard_map/ppermute | solution.py:343
  13.5 16.7 %copy-start = (bf16[128,216]{0,1:T(8,128)(2,1)S(1)}, bf16[128,216]{0,1:T(8,128)(2,1)}, u32[]{:S(2)}) copy-start(bf16[128,216]{0,1:T(8,128)(2,1)} %param.8) | copy-start | bytes 165892
  14.3 8.3 %collective-permute-start.2 = (bf16[48,1024]{1,0:T(8,128)(2,1)S(1)}, bf16[48,1024]{1,0:T(8,128)(2,1)S(1)}, u32[]{:S(2)}, u32[]{:S(2)}) collective-permute-start(bf16[48,1024]{1,0:T(8,128)(2,1)S(1)} %get-tuple-element.27), channel_id=1, source_target_pairs={{1,8},{3,10},{5,12},{7,14},{8,1},{9,64},{10,3},{11,66},{12,5},{13,... | collective-permute-start | bytes 294920 | tf_op jit(solution)/shard_map/ppermute | solution.py:343
  16.3 6.4 %collective-permute-start.3 = (bf16[48,1024]{1,0:T(8,128)(2,1)S(1)}, bf16[48,1024]{1,0:T(8,128)(2,1)S(1)}, u32[]{:S(2)}, u32[]{:S(2)}) collective-permute-start(bf16[48,1024]{1,0:T(8,128)(2,1)S(1)} %get-tuple-element.28), channel_id=1, source_target_pairs={{0,1},{1,0},{2,3},{3,2},{4,5},{5,4},{6,7},{7,6},{8,9},{9,8},{10,11... | collective-permute-start | bytes 294920 | tf_op jit(solution)/shard_map/ppermute | solution.py:343
  23.6 12.0 %collective-permute-start.4 = (bf16[64,1024]{1,0:T(8,128)(2,1)S(1)}, bf16[64,1024]{1,0:T(8,128)(2,1)S(1)}, u32[]{:S(2)}, u32[]{:S(2)}) collective-permute-start(bf16[64,1024]{1,0:T(8,128)(2,1)S(1)} %get-tuple-element.31), channel_id=1, source_target_pairs={{0,2},{1,3},{2,0},{3,1},{4,6},{5,7},{6,4},{7,5},{8,10},{9,11},{10,... | collective-permute-start | bytes 393224 | tf_op jit(solution)/shard_map/ppermute | solution.py:343
  24.4 11.2 %collective-permute-start.5 = (bf16[64,1024]{1,0:T(8,128)(2,1)S(1)}, bf16[64,1024]{1,0:T(8,128)(2,1)S(1)}, u32[]{:S(2)}, u32[]{:S(2)}) collective-permute-start(bf16[64,1024]{1,0:T(8,128)(2,1)S(1)} %get-tuple-element.32), channel_id=1, source_target_pairs={{2,16},{3,17},{6,20},{7,21},{10,24},{11,25},{14,28},{15,29},{16,2}... | collective-permute-start | bytes 393224 | tf_op jit(solution)/shard_map/ppermute | solution.py:343

commit v2 on v1

--- a/solution.py
+++ b/solution.py
@@ -16,7 +16,7 @@
 Y_BASE = X_BASE + 2 * X_ROWS
 Z_BASE = Y_BASE + 2 * Y_ROWS
 TABLE = Z_BASE + 2 * Z_ROWS
-PIECES = 4
+FIRST_FLOPS = 1 << 34
 Y_TABLE, Z_TABLE, LEVEL_TABLE, SIDE_TABLE, OUTER_TABLE, ORDER_TABLE = 0, 96, 224, 480, 992, 1376
 
 OFFSETS = [
@@ -137,26 +137,12 @@
     pick(even[0], sent, X_ROWS, to_even, to_odd)
 
 
-def stage_kernel(own, ops_hbm, table_hbm, ops, table, token, sem):
-    pieces = [(table_hbm, table)]
-    size = ops.shape[0] // PIECES
-    for piece in range(PIECES):
-        here = pl.ds(piece * size, size)
-        pieces.append((ops_hbm.at[here], ops.at[here]))
-    copies = [pltpu.make_async_copy(*piece, sem.at[i]) for i, piece in enumerate(pieces)]
-    for copy in copies:
-        copy.start()
-    token[...] = jnp.zeros_like(token)
-    for copy in copies:
-        copy.wait()
-
-
 def forward(table, own, landed, sent):
     width = OWN + landed.shape[0]
     sent[...] = (matmul(table[:, :OWN], own[...]) + matmul(table[:, OWN:width], landed[...])).astype(BF)
 
 
-def forward_y_kernel(even, own, xe, xo, table, token, to_even, to_odd, landed, sent):
+def forward_y_kernel(even, own, xe, xo, table, to_even, to_odd, landed, sent):
     place(even[0], xe, xo, X_ROWS, landed)
     forward(table.at[Y_TABLE:Z_TABLE], own, landed, sent)
     pick(even[1], sent, Y_ROWS, to_even, to_odd)
@@ -376,25 +362,16 @@
             pltpu.SemaphoreType.DMA((2,)),
         ],
         [SMEM] + [ANY] * 2,
+        flops=FIRST_FLOPS,
     )(even, in_hbm(multipoles), in_hbm(compress))
     x_pair = swap(send, bit_lists[0], device_count)
-    ops, table, token = call(
-        stage_kernel,
-        [
-            pltpu.VMEM(flat.shape, BF),
-            pltpu.VMEM(table.shape, BF),
-            pltpu.VMEM((8, RANK), F32),
-        ],
-        [pltpu.SemaphoreType.DMA((1 + PIECES,))],
-        [VMEM, ANY, ANY],
-        bytes_moved=flat.size * 4,
-    )(own, in_hbm(flat), in_hbm(table))
+    ops = flat
     *send, landed = call(
         forward_y_kernel,
         pair(Y_ROWS) + [pltpu.VMEM((2 * X_ROWS, 8 * RANK), BF)],
         [scratch(2 * Y_ROWS, 8 * RANK)],
-        [SMEM] + [VMEM] * 5,
-    )(even, own, *x_pair, table, token)
+        [SMEM] + [VMEM] * 4,
+    )(even, own, *x_pair, table)
     y_pair = swap(send, bit_lists[1], device_count)
     sums = (4, 4, 32, 2 * RANK)
     level, token = call(

time: 40 us -> 39.7 us (level)
  the two profiles are of different devices: /device:TPU:70 before, /device:TPU:98 now
where the time goes in v2:
time: 39.7 us; the launch traced here: 39.5 us
  Pallas kernels  16.4 us (41%)
  starting transfers between devices  16 us (40%)
  waiting for transfers between devices  6.88 us (17%)
    ppermute x6, starting transfers between devices, swap(): result.append(lax.ppermute(block, 'cells', route))  16 us
    ppermute x6, waiting for transfers between devices, swap(): result.append(lax.ppermute(block, 'cells', route))  6.88 us
    pallas_call x1, Pallas kernels, local(): call(side_kernel, [pltpu.VMEM(sums, F32), pltpu.VMEM(expand.shape[::-1],...  5.39 us
    pallas_call x1, Pallas kernels, local(): call(outer_kernel, jax.ShapeDtypeStruct((expand.shape[1], multipoles.shap...  4.24 us
    pallas_call x1, Pallas kernels, local(): call(compress_kernel, [pltpu.VMEM((OWN, 8 * RANK), BF)] + pair(X_ROWS), [...  2.65 us
    pallas_call x1, Pallas kernels, local(): call(level_kernel, [pltpu.VMEM(sums, F32), pltpu.VMEM((8, RANK), F32)], [...  2.48 us
    pallas_call x1, Pallas kernels, local(): call(forward_z_kernel, pair(Z_ROWS) + [pltpu.VMEM((Z_BASE - OWN, 8 * RANK...  0.86 us
    pallas_call x1, Pallas kernels, local(): call(forward_y_kernel, pair(Y_ROWS) + [pltpu.VMEM((2 * X_ROWS, 8 * RANK),...  0.81 us
  transfers between devices with their start and end apart: 6, of which 3 were waited for; matrix products, arithmetic and copies ran while one was open for 0% of the time, Pallas kernels for 20%

profile of v2, /device:TPU:98, one launch (start us, length us, event | category | flops | bytes accessed | tf_op | source)
XLA Modules:
  0.0 39.5 jit_solution(12305386637465106603)
XLA Ops:
  0.0 0.1 pad_add_fusion.even
  0.1 0.0 copy-start.1
  0.1 0.0 copy-start
  0.1 2.7 %shard_map.55 = (bf16[128,1024]{1,0:T(8,128)(2,1)S(1)}, bf16[16,1024]{1,0:T(8,128)(2,1)S(1)}, bf16[16,1024]{1,0:T(8,128)(2,1)S(1)}) custom-call(s32[3]{0:T(128)S(1)} %pad_add_fusion.even, bf16[216,1024]{1,0:T(8,128)(2,1)} %multipoles_hbm.1, bf16[216,128]{1,0:T(8,128)(2,1)} %compress_hbm.1), custom_call_target="tpu_custom_call" | custom-call | flops 17179869184 | bytes 1048576 | tf_op jit(solution)/shard_map/pallas_call | solution.py:354
  2.7 0.0 copy-start.2
  2.8 2.2 %collective-permute-start = (bf16[16,1024]{1,0:T(8,128)(2,1)S(1)}, bf16[16,1024]{1,0:T(8,128)(2,1)S(1)}, u32[]{:S(2)}, u32[]{:S(2)}) collective-permute-start(bf16[16,1024]{1,0:T(8,128)(2,1)S(1)} %get-tuple-element.19), channel_id=1, source_target_pairs={{0,4},{1,5},{2,6},{3,7},{4,0},{5,1},{6,2},{7,3},{8,12},{9,13},{10,... | collective-permute-start | bytes 98312 | tf_op jit(solution)/shard_map/ppermute | solution.py:329
  5.0 3.1 %collective-permute-start.1 = (bf16[16,1024]{1,0:T(8,128)(2,1)S(1)}, bf16[16,1024]{1,0:T(8,128)(2,1)S(1)}, u32[]{:S(2)}, u32[]{:S(2)}) collective-permute-start(bf16[16,1024]{1,0:T(8,128)(2,1)S(1)} %get-tuple-element.20), channel_id=1, source_target_pairs={{4,32},{5,33},{6,34},{7,35},{12,40},{13,41},{14,42},{15,43},{20,48... | collective-permute-start | bytes 98312 | tf_op jit(solution)/shard_map/ppermute | solution.py:329
  8.1 0.1 collective-permute-done.xe
  8.2 4.9 %collective-permute-done.1.xo = bf16[16,1024]{1,0:T(8,128)(2,1)S(1)} collective-permute-done((bf16[16,1024]{1,0:T(8,128)(2,1)S(1)}, bf16[16,1024]{1,0:T(8,128)(2,1)S(1)}, u32[]{:S(2)}, u32[]{:S(2)}) %collective-permute-start.1) | collective-permute-done | bytes 32800 | tf_op jit(solution)/shard_map/ppermute | solution.py:329
  13.2 0.0 copy-done.1
  13.2 0.8 %shard_map.56 = (bf16[48,1024]{1,0:T(8,128)(2,1)S(1)}, bf16[48,1024]{1,0:T(8,128)(2,1)S(1)}, bf16[32,1024]{1,0:T(8,128)(2,1)S(1)}) custom-call(s32[3]{0:T(128)S(1)} %pad_add_fusion.even, bf16[128,1024]{1,0:T(8,128)(2,1)S(1)} %get-tuple-element.18.own, bf16[16,1024]{1,0:T(8,128)(2,1)S(1)} %collective-permute-done.xe, ...), custom_call_target="tpu_custom_call" | custom-call | flops 16777216 | bytes 1048576 | tf_op jit(solution)/shard_map/pallas_call | solution.py:369
  14.0 1.9 %collective-permute-start.2 = (bf16[48,1024]{1,0:T(8,128)(2,1)S(1)}, bf16[48,1024]{1,0:T(8,128)(2,1)S(1)}, u32[]{:S(2)}, u32[]{:S(2)}) collective-permute-start(bf16[48,1024]{1,0:T(8,128)(2,1)S(1)} %get-tuple-element.22), channel_id=1, source_target_pairs={{1,8},{3,10},{5,12},{7,14},{8,1},{9,64},{10,3},{11,66},{12,5},{13,... | collective-permute-start | bytes 294920 | tf_op jit(solution)/shard_map/ppermute | solution.py:329
  15.9 2.1 %collective-permute-start.3 = (bf16[48,1024]{1,0:T(8,128)(2,1)S(1)}, bf16[48,1024]{1,0:T(8,128)(2,1)S(1)}, u32[]{:S(2)}, u32[]{:S(2)}) collective-permute-start(bf16[48,1024]{1,0:T(8,128)(2,1)S(1)} %get-tuple-element.23), channel_id=1, source_target_pairs={{0,1},{1,0},{2,3},{3,2},{4,5},{5,4},{6,7},{7,6},{8,9},{9,8},{10,11... | collective-permute-start | bytes 294920 | tf_op jit(solution)/shard_map/ppermute | solution.py:329
  18.0 0.0 copy-done
  18.0 2.5 %shard_map.57 = (f32[4,4,32,256]{3,2,1,0:T(8,128)S(1)}, f32[8,128]{1,0:T(8,128)S(1)}) custom-call(bf16[128,1024]{1,0:T(8,128)(2,1)S(1)} %get-tuple-element.18.own, bf16[32,1024]{1,0:T(8,128)(2,1)S(1)} %get-tuple-element.21.landed.x_landed, bf16[1504,384]{1,0:T(8,128)(2,1)S(1)} %copy-done.1, bf16[40448,128]{1,0:T(8,128)(2,1)S(1)} %bitcast.5), custom_call_target="tpu_custom_call" | custom-call | flops 2147483648 | bytes 1048576 | tf_op jit(solution)/shard_map/pallas_call | solution.py:377
  20.5 1.8 %collective-permute-done.2.yo = bf16[48,1024]{1,0:T(8,128)(2,1)S(1)} collective-permute-done((bf16[48,1024]{1,0:T(8,128)(2,1)S(1)}, bf16[48,1024]{1,0:T(8,128)(2,1)S(1)}, u32[]{:S(2)}, u32[]{:S(2)}) %collective-permute-start.2) | collective-permute-done | bytes 98336 | tf_op jit(solution)/shard_map/ppermute | solution.py:329
  22.3 0.0 collective-permute-done.3.ye
  22.3 0.9 %shard_map.58 = (bf16[64,1024]{1,0:T(8,128)(2,1)S(1)}, bf16[64,1024]{1,0:T(8,128)(2,1)S(1)}, bf16[128,1024]{1,0:T(8,128)(2,1)S(1)}) custom-call(s32[3]{0:T(128)S(1)} %pad_add_fusion.even, bf16[128,1024]{1,0:T(8,128)(2,1)S(1)} %get-tuple-element.18.own, bf16[32,1024]{1,0:T(8,128)(2,1)S(1)} %get-tuple-element.21.landed.x_landed, ...), custom_call_target="tpu_custom_call" | custom-call | flops 16777216 | bytes 1048576 | tf_op jit(solution)/shard_map/pallas_call | solution.py:384
  23.2 1.5 %collective-permute-start.4 = (bf16[64,1024]{1,0:T(8,128)(2,1)S(1)}, bf16[64,1024]{1,0:T(8,128)(2,1)S(1)}, u32[]{:S(2)}, u32[]{:S(2)}) collective-permute-start(bf16[64,1024]{1,0:T(8,128)(2,1)S(1)} %get-tuple-element.25), channel_id=1, source_target_pairs={{0,2},{1,3},{2,0},{3,1},{4,6},{5,7},{6,4},{7,5},{8,10},{9,11},{10,... | collective-permute-start | bytes 393224 | tf_op jit(solution)/shard_map/ppermute | solution.py:329
  24.7 5.1 %collective-permute-start.5 = (bf16[64,1024]{1,0:T(8,128)(2,1)S(1)}, bf16[64,1024]{1,0:T(8,128)(2,1)S(1)}, u32[]{:S(2)}, u32[]{:S(2)}) collective-permute-start(bf16[64,1024]{1,0:T(8,128)(2,1)S(1)} %get-tuple-element.26), channel_id=1, source_target_pairs={{2,16},{3,17},{6,20},{7,21},{10,24},{11,25},{14,28},{15,29},{16,2}... | collective-permute-start | bytes 393224 | tf_op jit(solution)/shard_map/ppermute | solution.py:329
  29.8 0.0 copy-done.2
  29.8 5.4 %shard_map.59 = (f32[4,4,32,256]{3,2,1,0:T(8,128)S(1)}, bf16[216,128]{1,0:T(8,128)(2,1)S(1)}) custom-call(bf16[128,1024]{1,0:T(8,128)(2,1)S(1)} %get-tuple-element.18.own, bf16[128,1024]{1,0:T(8,128)(2,1)S(1)} %get-tuple-element.27.landed, bf16[1504,384]{1,0:T(8,128)(2,1)S(1)} %copy-done.1, bf16[216,128]{1,0:T(8,128)(2,1)S(1)} %bitcast.8, ...), custom_call_target="tpu_custom_call" | custom-call | flops 5368709120 | bytes 1048576 | tf_op jit(solution)/shard_map/pallas_call | solution.py:391
  35.2 0.0 collective-permute-done.4.ze
  35.3 0.0 collective-permute-done.5.zo
  35.3 4.2 %shard_map.60 = f32[216,1024]{1,0:T(8,128)} custom-call(s32[3]{0:T(128)S(1)} %pad_add_fusion.even, bf16[64,1024]{1,0:T(8,128)(2,1)S(1)} %collective-permute-done.4.ze, bf16[64,1024]{1,0:T(8,128)(2,1)S(1)} %collective-permute-done.5.zo, bf16[1504,384]{1,0:T(8,128)(2,1)S(1)} %copy-done.1, bf16[216,128]{1,0:T(8,128)(2,1)S(1)} %get-tuple-element.29.expand, ...), custom_call_target="tpu_custom_call" | custom-call | flops 2147483648 | bytes 1048576 | tf_op jit(solution)/shard_map/pallas_call | solution.py:398
Async XLA Ops:
  0.1 13.1 %copy-start.1 = (bf16[1504,384]{1,0:T(8,128)(2,1)S(1)}, bf16[1504,384]{1,0:T(8,128)(2,1)}, u32[]{:S(2)}) copy-start(bf16[1504,384]{1,0:T(8,128)(2,1)} %constant.12.clone.table) | copy-start | bytes 3465220
  0.1 17.9 %copy-start = (bf16[316,128,128]{2,1,0:T(8,128)(2,1)S(1)}, bf16[316,128,128]{2,1,0:T(8,128)(2,1)}, u32[]{:S(2)}) copy-start(bf16[316,128,128]{2,1,0:T(8,128)(2,1)} %param.7) | copy-start | bytes 31064068
  2.7 27.1 %copy-start.2 = (bf16[128,216]{0,1:T(8,128)(2,1)S(1)}, bf16[128,216]{0,1:T(8,128)(2,1)}, u32[]{:S(2)}) copy-start(bf16[128,216]{0,1:T(8,128)(2,1)} %param.8) | copy-start | bytes 165892
  2.8 5.5 %collective-permute-start = (bf16[16,1024]{1,0:T(8,128)(2,1)S(1)}, bf16[16,1024]{1,0:T(8,128)(2,1)S(1)}, u32[]{:S(2)}, u32[]{:S(2)}) collective-permute-start(bf16[16,1024]{1,0:T(8,128)(2,1)S(1)} %get-tuple-element.19), channel_id=1, source_target_pairs={{0,4},{1,5},{2,6},{3,7},{4,0},{5,1},{6,2},{7,3},{8,12},{9,13},{10,... | collective-permute-start | bytes 98312 | tf_op jit(solution)/shard_map/ppermute | solution.py:329
  5.0 8.2 %collective-permute-start.1 = (bf16[16,1024]{1,0:T(8,128)(2,1)S(1)}, bf16[16,1024]{1,0:T(8,128)(2,1)S(1)}, u32[]{:S(2)}, u32[]{:S(2)}) collective-permute-start(bf16[16,1024]{1,0:T(8,128)(2,1)S(1)} %get-tuple-element.20), channel_id=1, source_target_pairs={{4,32},{5,33},{6,34},{7,35},{12,40},{13,41},{14,42},{15,43},{20,48... | collective-permute-start | bytes 98312 | tf_op jit(solution)/shard_map/ppermute | solution.py:329
  14.0 8.3 %collective-permute-start.2 = (bf16[48,1024]{1,0:T(8,128)(2,1)S(1)}, bf16[48,1024]{1,0:T(8,128)(2,1)S(1)}, u32[]{:S(2)}, u32[]{:S(2)}) collective-permute-start(bf16[48,1024]{1,0:T(8,128)(2,1)S(1)} %get-tuple-element.22), channel_id=1, source_target_pairs={{1,8},{3,10},{5,12},{7,14},{8,1},{9,64},{10,3},{11,66},{12,5},{13,... | collective-permute-start | bytes 294920 | tf_op jit(solution)/shard_map/ppermute | solution.py:329
  15.9 6.4 %collective-permute-start.3 = (bf16[48,1024]{1,0:T(8,128)(2,1)S(1)}, bf16[48,1024]{1,0:T(8,128)(2,1)S(1)}, u32[]{:S(2)}, u32[]{:S(2)}) collective-permute-start(bf16[48,1024]{1,0:T(8,128)(2,1)S(1)} %get-tuple-element.23), channel_id=1, source_target_pairs={{0,1},{1,0},{2,3},{3,2},{4,5},{5,4},{6,7},{7,6},{8,9},{9,8},{10,11... | collective-permute-start | bytes 294920 | tf_op jit(solution)/shard_map/ppermute | solution.py:329
  23.2 12.1 %collective-permute-start.4 = (bf16[64,1024]{1,0:T(8,128)(2,1)S(1)}, bf16[64,1024]{1,0:T(8,128)(2,1)S(1)}, u32[]{:S(2)}, u32[]{:S(2)}) collective-permute-start(bf16[64,1024]{1,0:T(8,128)(2,1)S(1)} %get-tuple-element.25), channel_id=1, source_target_pairs={{0,2},{1,3},{2,0},{3,1},{4,6},{5,7},{6,4},{7,5},{8,10},{9,11},{10,... | collective-permute-start | bytes 393224 | tf_op jit(solution)/shard_map/ppermute | solution.py:329
  24.7 10.6 %collective-permute-start.5 = (bf16[64,1024]{1,0:T(8,128)(2,1)S(1)}, bf16[64,1024]{1,0:T(8,128)(2,1)S(1)}, u32[]{:S(2)}, u32[]{:S(2)}) collective-permute-start(bf16[64,1024]{1,0:T(8,128)(2,1)S(1)} %get-tuple-element.26), channel_id=1, source_target_pairs={{2,16},{3,17},{6,20},{7,21},{10,24},{11,25},{14,28},{15,29},{16,2}... | collective-permute-start | bytes 393224 | tf_op jit(solution)/shard_map/ppermute | solution.py:329

commit v3 on v2

--- a/solution.py
+++ b/solution.py
@@ -142,7 +142,7 @@
     sent[...] = (matmul(table[:, :OWN], own[...]) + matmul(table[:, OWN:width], landed[...])).astype(BF)
 
 
-def forward_y_kernel(even, own, xe, xo, table, to_even, to_odd, landed, sent):
+def forward_y_kernel(even, own, xo, xe, table, to_even, to_odd, landed, sent):
     place(even[0], xe, xo, X_ROWS, landed)
     forward(table.at[Y_TABLE:Z_TABLE], own, landed, sent)
     pick(even[1], sent, Y_ROWS, to_even, to_odd)
@@ -371,7 +371,7 @@
         pair(Y_ROWS) + [pltpu.VMEM((2 * X_ROWS, 8 * RANK), BF)],
         [scratch(2 * Y_ROWS, 8 * RANK)],
         [SMEM] + [VMEM] * 4,
-    )(even, own, *x_pair, table)
+    )(even, own, *x_pair[::-1], table)
     y_pair = swap(send, bit_lists[1], device_count)
     sums = (4, 4, 32, 2 * RANK)
     level, token = call(

time: 39.7 us -> 39.4 us (level)
  the two profiles are of different devices: /device:TPU:98 before, /device:TPU:70 now
where the time goes in v3:
time: 39.4 us; the launch traced here: 39.2 us
  Pallas kernels  16.4 us (42%)
  starting transfers between devices  15 us (38%)
  waiting for transfers between devices  7.57 us (19%)
    ppermute x6, starting transfers between devices, swap(): result.append(lax.ppermute(block, 'cells', route))  15 us
    ppermute x6, waiting for transfers between devices, swap(): result.append(lax.ppermute(block, 'cells', route))  7.57 us
    pallas_call x1, Pallas kernels, local(): call(side_kernel, [pltpu.VMEM(sums, F32), pltpu.VMEM(expand.shape[::-1],...  5.39 us
    pallas_call x1, Pallas kernels, local(): call(outer_kernel, jax.ShapeDtypeStruct((expand.shape[1], multipoles.shap...  4.24 us
    pallas_call x1, Pallas kernels, local(): call(compress_kernel, [pltpu.VMEM((OWN, 8 * RANK), BF)] + pair(X_ROWS), [...  2.65 us
    pallas_call x1, Pallas kernels, local(): call(level_kernel, [pltpu.VMEM(sums, F32), pltpu.VMEM((8, RANK), F32)], [...  2.49 us
    pallas_call x1, Pallas kernels, local(): call(forward_z_kernel, pair(Z_ROWS) + [pltpu.VMEM((Z_BASE - OWN, 8 * RANK...  0.86 us
    pallas_call x1, Pallas kernels, local(): call(forward_y_kernel, pair(Y_ROWS) + [pltpu.VMEM((2 * X_ROWS, 8 * RANK),...  0.81 us
  transfers between devices with their start and end apart: 6, of which 3 were waited for; matrix products, arithmetic and copies ran while one was open for 0% of the time, Pallas kernels for 20%

profile of v3, /device:TPU:70, one launch (start us, length us, event | category | flops | bytes accessed | tf_op | source)
XLA Modules:
  0.0 39.2 jit_solution(2779173688998946710)
XLA Ops:
  0.0 0.1 pad_add_fusion.even
  0.1 0.0 copy-start.1
  0.1 0.0 copy-start
  0.1 2.7 %shard_map.55 = (bf16[128,1024]{1,0:T(8,128)(2,1)S(1)}, bf16[16,1024]{1,0:T(8,128)(2,1)S(1)}, bf16[16,1024]{1,0:T(8,128)(2,1)S(1)}) custom-call(s32[3]{0:T(128)S(1)} %pad_add_fusion.even, bf16[216,1024]{1,0:T(8,128)(2,1)} %multipoles_hbm.1, bf16[216,128]{1,0:T(8,128)(2,1)} %compress_hbm.1), custom_call_target="tpu_custom_call" | custom-call | flops 17179869184 | bytes 1048576 | tf_op jit(solution)/shard_map/pallas_call | solution.py:354
  2.7 0.0 copy-start.2
  2.8 4.6 %collective-permute-start = (bf16[16,1024]{1,0:T(8,128)(2,1)S(1)}, bf16[16,1024]{1,0:T(8,128)(2,1)S(1)}, u32[]{:S(2)}, u32[]{:S(2)}) collective-permute-start(bf16[16,1024]{1,0:T(8,128)(2,1)S(1)} %get-tuple-element.19), channel_id=1, source_target_pairs={{4,32},{5,33},{6,34},{7,35},{12,40},{13,41},{14,42},{15,43},{20,48... | collective-permute-start | bytes 98312 | tf_op jit(solution)/shard_map/ppermute | solution.py:329
  7.4 0.1 collective-permute-start.1
  7.5 3.7 %collective-permute-done.xo = bf16[16,1024]{1,0:T(8,128)(2,1)S(1)} collective-permute-done((bf16[16,1024]{1,0:T(8,128)(2,1)S(1)}, bf16[16,1024]{1,0:T(8,128)(2,1)S(1)}, u32[]{:S(2)}, u32[]{:S(2)}) %collective-permute-start) | collective-permute-done | bytes 32800 | tf_op jit(solution)/shard_map/ppermute | solution.py:329
  11.2 1.7 %collective-permute-done.1.xe = bf16[16,1024]{1,0:T(8,128)(2,1)S(1)} collective-permute-done((bf16[16,1024]{1,0:T(8,128)(2,1)S(1)}, bf16[16,1024]{1,0:T(8,128)(2,1)S(1)}, u32[]{:S(2)}, u32[]{:S(2)}) %collective-permute-start.1) | collective-permute-done | bytes 32800 | tf_op jit(solution)/shard_map/ppermute | solution.py:329
  12.9 0.0 copy-done.1
  12.9 0.8 %shard_map.56 = (bf16[48,1024]{1,0:T(8,128)(2,1)S(1)}, bf16[48,1024]{1,0:T(8,128)(2,1)S(1)}, bf16[32,1024]{1,0:T(8,128)(2,1)S(1)}) custom-call(s32[3]{0:T(128)S(1)} %pad_add_fusion.even, bf16[128,1024]{1,0:T(8,128)(2,1)S(1)} %get-tuple-element.18.own, bf16[16,1024]{1,0:T(8,128)(2,1)S(1)} %collective-permute-done.xo, ...), custom_call_target="tpu_custom_call" | custom-call | flops 16777216 | bytes 1048576 | tf_op jit(solution)/shard_map/pallas_call | solution.py:369
  13.7 1.9 %collective-permute-start.2 = (bf16[48,1024]{1,0:T(8,128)(2,1)S(1)}, bf16[48,1024]{1,0:T(8,128)(2,1)S(1)}, u32[]{:S(2)}, u32[]{:S(2)}) collective-permute-start(bf16[48,1024]{1,0:T(8,128)(2,1)S(1)} %get-tuple-element.22), channel_id=1, source_target_pairs={{1,8},{3,10},{5,12},{7,14},{8,1},{9,64},{10,3},{11,66},{12,5},{13,... | collective-permute-start | bytes 294920 | tf_op jit(solution)/shard_map/ppermute | solution.py:329
  15.6 1.8 %collective-permute-start.3 = (bf16[48,1024]{1,0:T(8,128)(2,1)S(1)}, bf16[48,1024]{1,0:T(8,128)(2,1)S(1)}, u32[]{:S(2)}, u32[]{:S(2)}) collective-permute-start(bf16[48,1024]{1,0:T(8,128)(2,1)S(1)} %get-tuple-element.23), channel_id=1, source_target_pairs={{0,1},{1,0},{2,3},{3,2},{4,5},{5,4},{6,7},{7,6},{8,9},{9,8},{10,11... | collective-permute-start | bytes 294920 | tf_op jit(solution)/shard_map/ppermute | solution.py:329
  17.4 0.0 copy-done
  17.4 2.5 %shard_map.57 = (f32[4,4,32,256]{3,2,1,0:T(8,128)S(1)}, f32[8,128]{1,0:T(8,128)S(1)}) custom-call(bf16[128,1024]{1,0:T(8,128)(2,1)S(1)} %get-tuple-element.18.own, bf16[32,1024]{1,0:T(8,128)(2,1)S(1)} %get-tuple-element.21.landed.x_landed, bf16[1504,384]{1,0:T(8,128)(2,1)S(1)} %copy-done.1, bf16[40448,128]{1,0:T(8,128)(2,1)S(1)} %bitcast.5), custom_call_target="tpu_custom_call" | custom-call | flops 2147483648 | bytes 1048576 | tf_op jit(solution)/shard_map/pallas_call | solution.py:377
  19.9 2.2 %collective-permute-done.2.yo = bf16[48,1024]{1,0:T(8,128)(2,1)S(1)} collective-permute-done((bf16[48,1024]{1,0:T(8,128)(2,1)S(1)}, bf16[48,1024]{1,0:T(8,128)(2,1)S(1)}, u32[]{:S(2)}, u32[]{:S(2)}) %collective-permute-start.2) | collective-permute-done | bytes 98336 | tf_op jit(solution)/shard_map/ppermute | solution.py:329
  22.1 0.0 collective-permute-done.3.ye
  22.1 0.9 %shard_map.58 = (bf16[64,1024]{1,0:T(8,128)(2,1)S(1)}, bf16[64,1024]{1,0:T(8,128)(2,1)S(1)}, bf16[128,1024]{1,0:T(8,128)(2,1)S(1)}) custom-call(s32[3]{0:T(128)S(1)} %pad_add_fusion.even, bf16[128,1024]{1,0:T(8,128)(2,1)S(1)} %get-tuple-element.18.own, bf16[32,1024]{1,0:T(8,128)(2,1)S(1)} %get-tuple-element.21.landed.x_landed, ...), custom_call_target="tpu_custom_call" | custom-call | flops 16777216 | bytes 1048576 | tf_op jit(solution)/shard_map/pallas_call | solution.py:384
  22.9 0.1 collective-permute-start.4
  23.0 6.5 %collective-permute-start.5 = (bf16[64,1024]{1,0:T(8,128)(2,1)S(1)}, bf16[64,1024]{1,0:T(8,128)(2,1)S(1)}, u32[]{:S(2)}, u32[]{:S(2)}) collective-permute-start(bf16[64,1024]{1,0:T(8,128)(2,1)S(1)} %get-tuple-element.26), channel_id=1, source_target_pairs={{2,16},{3,17},{6,20},{7,21},{10,24},{11,25},{14,28},{15,29},{16,2}... | collective-permute-start | bytes 393224 | tf_op jit(solution)/shard_map/ppermute | solution.py:329
  29.6 0.0 copy-done.2
  29.6 5.4 %shard_map.59 = (f32[4,4,32,256]{3,2,1,0:T(8,128)S(1)}, bf16[216,128]{1,0:T(8,128)(2,1)S(1)}) custom-call(bf16[128,1024]{1,0:T(8,128)(2,1)S(1)} %get-tuple-element.18.own, bf16[128,1024]{1,0:T(8,128)(2,1)S(1)} %get-tuple-element.27.landed, bf16[1504,384]{1,0:T(8,128)(2,1)S(1)} %copy-done.1, bf16[216,128]{1,0:T(8,128)(2,1)S(1)} %bitcast.8, ...), custom_call_target="tpu_custom_call" | custom-call | flops 5368709120 | bytes 1048576 | tf_op jit(solution)/shard_map/pallas_call | solution.py:391
  35.0 0.0 collective-permute-done.4.ze
  35.0 0.0 collective-permute-done.5.zo
  35.0 4.2 %shard_map.60 = f32[216,1024]{1,0:T(8,128)} custom-call(s32[3]{0:T(128)S(1)} %pad_add_fusion.even, bf16[64,1024]{1,0:T(8,128)(2,1)S(1)} %collective-permute-done.4.ze, bf16[64,1024]{1,0:T(8,128)(2,1)S(1)} %collective-permute-done.5.zo, bf16[1504,384]{1,0:T(8,128)(2,1)S(1)} %copy-done.1, bf16[216,128]{1,0:T(8,128)(2,1)S(1)} %get-tuple-element.29.expand, ...), custom_call_target="tpu_custom_call" | custom-call | flops 2147483648 | bytes 1048576 | tf_op jit(solution)/shard_map/pallas_call | solution.py:398
Async XLA Ops:
  0.1 12.8 %copy-start.1 = (bf16[1504,384]{1,0:T(8,128)(2,1)S(1)}, bf16[1504,384]{1,0:T(8,128)(2,1)}, u32[]{:S(2)}) copy-start(bf16[1504,384]{1,0:T(8,128)(2,1)} %constant.12.clone.table) | copy-start | bytes 3465220
  0.1 17.3 %copy-start = (bf16[316,128,128]{2,1,0:T(8,128)(2,1)S(1)}, bf16[316,128,128]{2,1,0:T(8,128)(2,1)}, u32[]{:S(2)}) copy-start(bf16[316,128,128]{2,1,0:T(8,128)(2,1)} %param.7) | copy-start | bytes 31064068
  2.7 26.8 %copy-start.2 = (bf16[128,216]{0,1:T(8,128)(2,1)S(1)}, bf16[128,216]{0,1:T(8,128)(2,1)}, u32[]{:S(2)}) copy-start(bf16[128,216]{0,1:T(8,128)(2,1)} %param.8) | copy-start | bytes 165892
  2.8 8.5 %collective-permute-start = (bf16[16,1024]{1,0:T(8,128)(2,1)S(1)}, bf16[16,1024]{1,0:T(8,128)(2,1)S(1)}, u32[]{:S(2)}, u32[]{:S(2)}) collective-permute-start(bf16[16,1024]{1,0:T(8,128)(2,1)S(1)} %get-tuple-element.19), channel_id=1, source_target_pairs={{4,32},{5,33},{6,34},{7,35},{12,40},{13,41},{14,42},{15,43},{20,48... | collective-permute-start | bytes 98312 | tf_op jit(solution)/shard_map/ppermute | solution.py:329
  7.4 5.5 %collective-permute-start.1 = (bf16[16,1024]{1,0:T(8,128)(2,1)S(1)}, bf16[16,1024]{1,0:T(8,128)(2,1)S(1)}, u32[]{:S(2)}, u32[]{:S(2)}) collective-permute-start(bf16[16,1024]{1,0:T(8,128)(2,1)S(1)} %get-tuple-element.20), channel_id=1, source_target_pairs={{0,4},{1,5},{2,6},{3,7},{4,0},{5,1},{6,2},{7,3},{8,12},{9,13},{10,... | collective-permute-start | bytes 98312 | tf_op jit(solution)/shard_map/ppermute | solution.py:329
  13.7 8.3 %collective-permute-start.2 = (bf16[48,1024]{1,0:T(8,128)(2,1)S(1)}, bf16[48,1024]{1,0:T(8,128)(2,1)S(1)}, u32[]{:S(2)}, u32[]{:S(2)}) collective-permute-start(bf16[48,1024]{1,0:T(8,128)(2,1)S(1)} %get-tuple-element.22), channel_id=1, source_target_pairs={{1,8},{3,10},{5,12},{7,14},{8,1},{9,64},{10,3},{11,66},{12,5},{13,... | collective-permute-start | bytes 294920 | tf_op jit(solution)/shard_map/ppermute | solution.py:329
  15.6 6.4 %collective-permute-start.3 = (bf16[48,1024]{1,0:T(8,128)(2,1)S(1)}, bf16[48,1024]{1,0:T(8,128)(2,1)S(1)}, u32[]{:S(2)}, u32[]{:S(2)}) collective-permute-start(bf16[48,1024]{1,0:T(8,128)(2,1)S(1)} %get-tuple-element.23), channel_id=1, source_target_pairs={{0,1},{1,0},{2,3},{3,2},{4,5},{5,4},{6,7},{7,6},{8,9},{9,8},{10,11... | collective-permute-start | bytes 294920 | tf_op jit(solution)/shard_map/ppermute | solution.py:329
  22.9 12.1 %collective-permute-start.4 = (bf16[64,1024]{1,0:T(8,128)(2,1)S(1)}, bf16[64,1024]{1,0:T(8,128)(2,1)S(1)}, u32[]{:S(2)}, u32[]{:S(2)}) collective-permute-start(bf16[64,1024]{1,0:T(8,128)(2,1)S(1)} %get-tuple-element.25), channel_id=1, source_target_pairs={{0,2},{1,3},{2,0},{3,1},{4,6},{5,7},{6,4},{7,5},{8,10},{9,11},{10,... | collective-permute-start | bytes 393224 | tf_op jit(solution)/shard_map/ppermute | solution.py:329
  23.0 12.0 %collective-permute-start.5 = (bf16[64,1024]{1,0:T(8,128)(2,1)S(1)}, bf16[64,1024]{1,0:T(8,128)(2,1)S(1)}, u32[]{:S(2)}, u32[]{:S(2)}) collective-permute-start(bf16[64,1024]{1,0:T(8,128)(2,1)S(1)} %get-tuple-element.26), channel_id=1, source_target_pairs={{2,16},{3,17},{6,20},{7,21},{10,24},{11,25},{14,28},{15,29},{16,2}... | collective-permute-start | bytes 393224 | tf_op jit(solution)/shard_map/ppermute | solution.py:329

commit v4 on v3

--- a/solution.py
+++ b/solution.py
@@ -255,7 +255,7 @@
     interact(source, ops, level, acc, ALL_PLANES, ALL_PAIRS, [-2, 2], ([-1, 3], [-3, 1]))
 
 
-def outer_kernel(even, ze, zo, table, expand, ops, inner, out, landed, window, acc, rows):
+def outer_kernel(even, zo, ze, table, expand, ops, inner, out, landed, window, acc, rows):
     place(even[2], ze, zo, Z_ROWS, landed)
     for px in range(4):
         block = table[OUTER_TABLE + px * 96 : OUTER_TABLE + px * 96 + 96, Z_BASE:]
@@ -406,7 +406,7 @@
         ],
         [SMEM] + [VMEM] * 6,
         flops=2 << 30,
-    )(even, *z_pair, table, expand_t, ops, inner)
+    )(even, *z_pair[::-1], table, expand_t, ops, inner)
 
 
 def solution(mesh):

time: 39.4 us -> 39.8 us (1.010)
  the two profiles are of different devices: /device:TPU:70 before, /device:TPU:96 now
where the time goes in v4:
time: 39.8 us; the launch traced here: 39.6 us
  Pallas kernels  16.4 us (41%)
  starting transfers between devices  15.4 us (39%)
  waiting for transfers between devices  7.57 us (19%)
    ppermute x6, starting transfers between devices, swap(): result.append(lax.ppermute(block, 'cells', route))  15.4 us
    ppermute x6, waiting for transfers between devices, swap(): result.append(lax.ppermute(block, 'cells', route))  7.57 us
    pallas_call x1, Pallas kernels, local(): call(side_kernel, [pltpu.VMEM(sums, F32), pltpu.VMEM(expand.shape[::-1],...  5.39 us
    pallas_call x1, Pallas kernels, local(): call(outer_kernel, jax.ShapeDtypeStruct((expand.shape[1], multipoles.shap...  4.24 us
    pallas_call x1, Pallas kernels, local(): call(compress_kernel, [pltpu.VMEM((OWN, 8 * RANK), BF)] + pair(X_ROWS), [...  2.65 us
    pallas_call x1, Pallas kernels, local(): call(level_kernel, [pltpu.VMEM(sums, F32), pltpu.VMEM((8, RANK), F32)], [...  2.49 us
    pallas_call x1, Pallas kernels, local(): call(forward_z_kernel, pair(Z_ROWS) + [pltpu.VMEM((Z_BASE - OWN, 8 * RANK...  0.86 us
    pallas_call x1, Pallas kernels, local(): call(forward_y_kernel, pair(Y_ROWS) + [pltpu.VMEM((2 * X_ROWS, 8 * RANK),...  0.81 us
  transfers between devices with their start and end apart: 6, of which 3 were waited for; matrix products, arithmetic and copies ran while one was open for 0% of the time, Pallas kernels for 20%

profile of v4, /device:TPU:96, one launch (start us, length us, event | category | flops | bytes accessed | tf_op | source)
XLA Modules:
  0.0 39.6 jit_solution(6259535837069435535)
XLA Ops:
  0.0 0.1 pad_add_fusion.even
  0.1 0.0 copy-start.1
  0.1 0.0 copy-start
  0.1 2.7 %shard_map.55 = (bf16[128,1024]{1,0:T(8,128)(2,1)S(1)}, bf16[16,1024]{1,0:T(8,128)(2,1)S(1)}, bf16[16,1024]{1,0:T(8,128)(2,1)S(1)}) custom-call(s32[3]{0:T(128)S(1)} %pad_add_fusion.even, bf16[216,1024]{1,0:T(8,128)(2,1)} %multipoles_hbm.1, bf16[216,128]{1,0:T(8,128)(2,1)} %compress_hbm.1), custom_call_target="tpu_custom_call" | custom-call | flops 17179869184 | bytes 1048576 | tf_op jit(solution)/shard_map/pallas_call | solution.py:354
  2.7 0.0 copy-start.2
  2.8 5.0 %collective-permute-start = (bf16[16,1024]{1,0:T(8,128)(2,1)S(1)}, bf16[16,1024]{1,0:T(8,128)(2,1)S(1)}, u32[]{:S(2)}, u32[]{:S(2)}) collective-permute-start(bf16[16,1024]{1,0:T(8,128)(2,1)S(1)} %get-tuple-element.19), channel_id=1, source_target_pairs={{4,32},{5,33},{6,34},{7,35},{12,40},{13,41},{14,42},{15,43},{20,48... | collective-permute-start | bytes 98312 | tf_op jit(solution)/shard_map/ppermute | solution.py:329
  7.8 0.1 collective-permute-start.1
  7.9 3.3 %collective-permute-done.xo = bf16[16,1024]{1,0:T(8,128)(2,1)S(1)} collective-permute-done((bf16[16,1024]{1,0:T(8,128)(2,1)S(1)}, bf16[16,1024]{1,0:T(8,128)(2,1)S(1)}, u32[]{:S(2)}, u32[]{:S(2)}) %collective-permute-start) | collective-permute-done | bytes 32800 | tf_op jit(solution)/shard_map/ppermute | solution.py:329
  11.2 2.1 %collective-permute-done.1.xe = bf16[16,1024]{1,0:T(8,128)(2,1)S(1)} collective-permute-done((bf16[16,1024]{1,0:T(8,128)(2,1)S(1)}, bf16[16,1024]{1,0:T(8,128)(2,1)S(1)}, u32[]{:S(2)}, u32[]{:S(2)}) %collective-permute-start.1) | collective-permute-done | bytes 32800 | tf_op jit(solution)/shard_map/ppermute | solution.py:329
  13.3 0.0 copy-done.1
  13.3 0.8 %shard_map.56 = (bf16[48,1024]{1,0:T(8,128)(2,1)S(1)}, bf16[48,1024]{1,0:T(8,128)(2,1)S(1)}, bf16[32,1024]{1,0:T(8,128)(2,1)S(1)}) custom-call(s32[3]{0:T(128)S(1)} %pad_add_fusion.even, bf16[128,1024]{1,0:T(8,128)(2,1)S(1)} %get-tuple-element.18.own, bf16[16,1024]{1,0:T(8,128)(2,1)S(1)} %collective-permute-done.xo, ...), custom_call_target="tpu_custom_call" | custom-call | flops 16777216 | bytes 1048576 | tf_op jit(solution)/shard_map/pallas_call | solution.py:369
  14.1 1.9 %collective-permute-start.2 = (bf16[48,1024]{1,0:T(8,128)(2,1)S(1)}, bf16[48,1024]{1,0:T(8,128)(2,1)S(1)}, u32[]{:S(2)}, u32[]{:S(2)}) collective-permute-start(bf16[48,1024]{1,0:T(8,128)(2,1)S(1)} %get-tuple-element.22), channel_id=1, source_target_pairs={{1,8},{3,10},{5,12},{7,14},{8,1},{9,64},{10,3},{11,66},{12,5},{13,... | collective-permute-start | bytes 294920 | tf_op jit(solution)/shard_map/ppermute | solution.py:329
  16.0 1.8 %collective-permute-start.3 = (bf16[48,1024]{1,0:T(8,128)(2,1)S(1)}, bf16[48,1024]{1,0:T(8,128)(2,1)S(1)}, u32[]{:S(2)}, u32[]{:S(2)}) collective-permute-start(bf16[48,1024]{1,0:T(8,128)(2,1)S(1)} %get-tuple-element.23), channel_id=1, source_target_pairs={{0,1},{1,0},{2,3},{3,2},{4,5},{5,4},{6,7},{7,6},{8,9},{9,8},{10,11... | collective-permute-start | bytes 294920 | tf_op jit(solution)/shard_map/ppermute | solution.py:329
  17.8 0.0 copy-done
  17.8 2.5 %shard_map.57 = (f32[4,4,32,256]{3,2,1,0:T(8,128)S(1)}, f32[8,128]{1,0:T(8,128)S(1)}) custom-call(bf16[128,1024]{1,0:T(8,128)(2,1)S(1)} %get-tuple-element.18.own, bf16[32,1024]{1,0:T(8,128)(2,1)S(1)} %get-tuple-element.21.landed.x_landed, bf16[1504,384]{1,0:T(8,128)(2,1)S(1)} %copy-done.1, bf16[40448,128]{1,0:T(8,128)(2,1)S(1)} %bitcast.5), custom_call_target="tpu_custom_call" | custom-call | flops 2147483648 | bytes 1048576 | tf_op jit(solution)/shard_map/pallas_call | solution.py:377
  20.3 2.2 %collective-permute-done.2.yo = bf16[48,1024]{1,0:T(8,128)(2,1)S(1)} collective-permute-done((bf16[48,1024]{1,0:T(8,128)(2,1)S(1)}, bf16[48,1024]{1,0:T(8,128)(2,1)S(1)}, u32[]{:S(2)}, u32[]{:S(2)}) %collective-permute-start.2) | collective-permute-done | bytes 98336 | tf_op jit(solution)/shard_map/ppermute | solution.py:329
  22.5 0.0 collective-permute-done.3.ye
  22.5 0.9 %shard_map.58 = (bf16[64,1024]{1,0:T(8,128)(2,1)S(1)}, bf16[64,1024]{1,0:T(8,128)(2,1)S(1)}, bf16[128,1024]{1,0:T(8,128)(2,1)S(1)}) custom-call(s32[3]{0:T(128)S(1)} %pad_add_fusion.even, bf16[128,1024]{1,0:T(8,128)(2,1)S(1)} %get-tuple-element.18.own, bf16[32,1024]{1,0:T(8,128)(2,1)S(1)} %get-tuple-element.21.landed.x_landed, ...), custom_call_target="tpu_custom_call" | custom-call | flops 16777216 | bytes 1048576 | tf_op jit(solution)/shard_map/pallas_call | solution.py:384
  23.3 0.7 %collective-permute-start.4 = (bf16[64,1024]{1,0:T(8,128)(2,1)S(1)}, bf16[64,1024]{1,0:T(8,128)(2,1)S(1)}, u32[]{:S(2)}, u32[]{:S(2)}) collective-permute-start(bf16[64,1024]{1,0:T(8,128)(2,1)S(1)} %get-tuple-element.25), channel_id=1, source_target_pairs={{2,16},{3,17},{6,20},{7,21},{10,24},{11,25},{14,28},{15,29},{16,2}... | collective-permute-start | bytes 393224 | tf_op jit(solution)/shard_map/ppermute | solution.py:329
  24.0 6.0 %collective-permute-start.5 = (bf16[64,1024]{1,0:T(8,128)(2,1)S(1)}, bf16[64,1024]{1,0:T(8,128)(2,1)S(1)}, u32[]{:S(2)}, u32[]{:S(2)}) collective-permute-start(bf16[64,1024]{1,0:T(8,128)(2,1)S(1)} %get-tuple-element.26), channel_id=1, source_target_pairs={{0,2},{1,3},{2,0},{3,1},{4,6},{5,7},{6,4},{7,5},{8,10},{9,11},{10,... | collective-permute-start | bytes 393224 | tf_op jit(solution)/shard_map/ppermute | solution.py:329
  30.0 0.0 copy-done.2
  30.0 5.4 %shard_map.59 = (f32[4,4,32,256]{3,2,1,0:T(8,128)S(1)}, bf16[216,128]{1,0:T(8,128)(2,1)S(1)}) custom-call(bf16[128,1024]{1,0:T(8,128)(2,1)S(1)} %get-tuple-element.18.own, bf16[128,1024]{1,0:T(8,128)(2,1)S(1)} %get-tuple-element.27.landed, bf16[1504,384]{1,0:T(8,128)(2,1)S(1)} %copy-done.1, bf16[216,128]{1,0:T(8,128)(2,1)S(1)} %bitcast.8, ...), custom_call_target="tpu_custom_call" | custom-call | flops 5368709120 | bytes 1048576 | tf_op jit(solution)/shard_map/pallas_call | solution.py:391
  35.4 0.0 collective-permute-done.4.zo
  35.4 0.0 collective-permute-done.5.ze
  35.4 4.2 %shard_map.60 = f32[216,1024]{1,0:T(8,128)} custom-call(s32[3]{0:T(128)S(1)} %pad_add_fusion.even, bf16[64,1024]{1,0:T(8,128)(2,1)S(1)} %collective-permute-done.4.zo, bf16[64,1024]{1,0:T(8,128)(2,1)S(1)} %collective-permute-done.5.ze, bf16[1504,384]{1,0:T(8,128)(2,1)S(1)} %copy-done.1, bf16[216,128]{1,0:T(8,128)(2,1)S(1)} %get-tuple-element.29.expand, ...), custom_call_target="tpu_custom_call" | custom-call | flops 2147483648 | bytes 1048576 | tf_op jit(solution)/shard_map/pallas_call | solution.py:398
Async XLA Ops:
  0.1 13.2 %copy-start.1 = (bf16[1504,384]{1,0:T(8,128)(2,1)S(1)}, bf16[1504,384]{1,0:T(8,128)(2,1)}, u32[]{:S(2)}) copy-start(bf16[1504,384]{1,0:T(8,128)(2,1)} %constant.12.clone.table) | copy-start | bytes 3465220
  0.1 17.7 %copy-start = (bf16[316,128,128]{2,1,0:T(8,128)(2,1)S(1)}, bf16[316,128,128]{2,1,0:T(8,128)(2,1)}, u32[]{:S(2)}) copy-start(bf16[316,128,128]{2,1,0:T(8,128)(2,1)} %param.7) | copy-start | bytes 31064068
  2.7 27.2 %copy-start.2 = (bf16[128,216]{0,1:T(8,128)(2,1)S(1)}, bf16[128,216]{0,1:T(8,128)(2,1)}, u32[]{:S(2)}) copy-start(bf16[128,216]{0,1:T(8,128)(2,1)} %param.8) | copy-start | bytes 165892
  2.8 8.5 %collective-permute-start = (bf16[16,1024]{1,0:T(8,128)(2,1)S(1)}, bf16[16,1024]{1,0:T(8,128)(2,1)S(1)}, u32[]{:S(2)}, u32[]{:S(2)}) collective-permute-start(bf16[16,1024]{1,0:T(8,128)(2,1)S(1)} %get-tuple-element.19), channel_id=1, source_target_pairs={{4,32},{5,33},{6,34},{7,35},{12,40},{13,41},{14,42},{15,43},{20,48... | collective-permute-start | bytes 98312 | tf_op jit(solution)/shard_map/ppermute | solution.py:329
  7.8 5.5 %collective-permute-start.1 = (bf16[16,1024]{1,0:T(8,128)(2,1)S(1)}, bf16[16,1024]{1,0:T(8,128)(2,1)S(1)}, u32[]{:S(2)}, u32[]{:S(2)}) collective-permute-start(bf16[16,1024]{1,0:T(8,128)(2,1)S(1)} %get-tuple-element.20), channel_id=1, source_target_pairs={{0,4},{1,5},{2,6},{3,7},{4,0},{5,1},{6,2},{7,3},{8,12},{9,13},{10,... | collective-permute-start | bytes 98312 | tf_op jit(solution)/shard_map/ppermute | solution.py:329
  14.1 8.3 %collective-permute-start.2 = (bf16[48,1024]{1,0:T(8,128)(2,1)S(1)}, bf16[48,1024]{1,0:T(8,128)(2,1)S(1)}, u32[]{:S(2)}, u32[]{:S(2)}) collective-permute-start(bf16[48,1024]{1,0:T(8,128)(2,1)S(1)} %get-tuple-element.22), channel_id=1, source_target_pairs={{1,8},{3,10},{5,12},{7,14},{8,1},{9,64},{10,3},{11,66},{12,5},{13,... | collective-permute-start | bytes 294920 | tf_op jit(solution)/shard_map/ppermute | solution.py:329
  16.0 6.4 %collective-permute-start.3 = (bf16[48,1024]{1,0:T(8,128)(2,1)S(1)}, bf16[48,1024]{1,0:T(8,128)(2,1)S(1)}, u32[]{:S(2)}, u32[]{:S(2)}) collective-permute-start(bf16[48,1024]{1,0:T(8,128)(2,1)S(1)} %get-tuple-element.23), channel_id=1, source_target_pairs={{0,1},{1,0},{2,3},{3,2},{4,5},{5,4},{6,7},{7,6},{8,9},{9,8},{10,11... | collective-permute-start | bytes 294920 | tf_op jit(solution)/shard_map/ppermute | solution.py:329
  23.3 12.1 %collective-permute-start.4 = (bf16[64,1024]{1,0:T(8,128)(2,1)S(1)}, bf16[64,1024]{1,0:T(8,128)(2,1)S(1)}, u32[]{:S(2)}, u32[]{:S(2)}) collective-permute-start(bf16[64,1024]{1,0:T(8,128)(2,1)S(1)} %get-tuple-element.25), channel_id=1, source_target_pairs={{2,16},{3,17},{6,20},{7,21},{10,24},{11,25},{14,28},{15,29},{16,2}... | collective-permute-start | bytes 393224 | tf_op jit(solution)/shard_map/ppermute | solution.py:329
  24.0 11.4 %collective-permute-start.5 = (bf16[64,1024]{1,0:T(8,128)(2,1)S(1)}, bf16[64,1024]{1,0:T(8,128)(2,1)S(1)}, u32[]{:S(2)}, u32[]{:S(2)}) collective-permute-start(bf16[64,1024]{1,0:T(8,128)(2,1)S(1)} %get-tuple-element.26), channel_id=1, source_target_pairs={{0,2},{1,3},{2,0},{3,1},{4,6},{5,7},{6,4},{7,5},{8,10},{9,11},{10,... | collective-permute-start | bytes 393224 | tf_op jit(solution)/shard_map/ppermute | solution.py:329
